TPU v7x, 32 devices: a whole 2x2x4 slice. The times are simulated.
32 devices in a mesh: fsdp: 16 (over z, x, core), tensor: 2 (over y).
Axes of the slice: x: 2, y: 2, z: 4, core: 2. Of those that a mesh axis runs over, the one named last changes fastest.
Arguments:
- tokens: bfloat16 [2, 3072, 1536], P(None, 'fsdp'), may hold values from -6 to 6
- norm1_gain: bfloat16 [1536], P('fsdp'), may hold values from 0.5 to 1.5
- query_weight: bfloat16 [1536, 1536], P('fsdp', 'tensor'), may hold values from -0.15625 to 0.15625
- query_bias: bfloat16 [12, 128], P('tensor'), may hold values from -3 to 3
- key_weight: bfloat16 [1536, 256], P('fsdp', 'tensor'), may hold values from -0.15625 to 0.15625
- key_bias: bfloat16 [2, 128], P('tensor'), may hold values from -3 to 3
- value_weight: bfloat16 [1536, 256], P('fsdp', 'tensor'), may hold values from -0.15625 to 0.15625
- value_bias: bfloat16 [2, 128], P('tensor'), may hold values from -3 to 3
- output_weight: bfloat16 [1536, 1536], P('tensor', 'fsdp'), may hold values from -0.625 to 0.625
- norm2_gain: bfloat16 [1536], P('fsdp'), may hold values from 0.5 to 1.5
- gate_weight: bfloat16 [1536, 8960], P('fsdp', 'tensor'), may hold values from -0.15625 to 0.15625
- up_weight: bfloat16 [1536, 8960], P('fsdp', 'tensor'), may hold values from -0.15625 to 0.15625
- down_weight: bfloat16 [8960, 1536], P('tensor', 'fsdp'), may hold values from -0.0625 to 0.0625
- cotangent: bfloat16 [2, 3072, 1536], P(None, 'fsdp'), may hold values from -6 to 6
- segments: int32 [2, 3072], replicated, may hold values from 0 to 107, as said below
- positions: int32 [2, 3072], replicated, may hold values from 0 to 799, as said below
Outputs:
- output: bfloat16 [2, 3072, 1536], P(None, 'fsdp')
- input_grad: float32 [2, 3072, 1536], P(None, 'fsdp')
- norm1_gain_grad: float32 [1536], P('fsdp')
- query_weight_grad: float32 [1536, 1536], P('fsdp', 'tensor')
- query_bias_grad: float32 [12, 128], P('tensor')
- key_weight_grad: float32 [1536, 256], P('fsdp', 'tensor')
- key_bias_grad: float32 [2, 128], P('tensor')
- value_weight_grad: float32 [1536, 256], P('fsdp', 'tensor')
- value_bias_grad: float32 [2, 128], P('tensor')
- output_weight_grad: float32 [1536, 1536], P('tensor', 'fsdp')
- norm2_gain_grad: float32 [1536], P('fsdp')
- gate_weight_grad: float32 [1536, 8960], P('fsdp', 'tensor')
- up_weight_grad: float32 [1536, 8960], P('fsdp', 'tensor')
- down_weight_grad: float32 [8960, 1536], P('tensor', 'fsdp')
Inputs may be any that keep to these rules, and one draw needn't show every extreme that they name: `segments`: along each micro-batch the numbers never fall; each number marks one document of consecutive tokens inside one sequence of 1024 tokens (sequences start at multiples of 1024); a document has at most 800 tokens, and some document has exactly 800; the documents of sequence j have numbers from j * (18) to (j + 1) * 18 - 1, the last document of each sequence the highest of these. `positions`: the position of each token within its document, counted from 0.
All inputs are finite; a program needn't handle non-finite values.
Results may differ from a plain program's by a relative error of at most 0.02.
Values may be sent and summed in bfloat16 or wider, within the bound.
A program may use at most 160 MiB of HBM per device.

v0:
```python
import functools
import math

import jax
import jax.numpy as jnp
from jax import lax
from jax.experimental import pallas as pl
from jax.experimental.pallas import tpu as pltpu
from jax.sharding import Mesh
from jax.sharding import PartitionSpec as P

BACK = 5
LINE = 4
LANES = 128
VMEM_BYTES = 63 * 1024 * 1024

EPSILON = 1e-06
THETA = 1000000.0
NEGATIVE = -1e30

RING, PAIR, CORE, TENSOR = "ring", "pair", "core", "tensor"
FSDP = (RING, PAIR, CORE)
SWAP = [(0, 1), (1, 0)]


def low(value):
    return value.astype(jnp.bfloat16)


def wide(value):
    return value.astype(jnp.float32)


def matmul(left_side, right_side):
    return jnp.dot(left_side, right_side, preferred_element_type=jnp.float32)


def contract_rows(left_side, right_side):
    return lax.dot_general(
        left_side, right_side, (((0,), (0,)), ((), ())), preferred_element_type=jnp.float32
    )


def times_transpose(left_side, right_side):
    return lax.dot_general(
        left_side, right_side, (((1,), (1,)), ((), ())), preferred_element_type=jnp.float32
    )


def swapped(value, axis):
    return lax.ppermute(value, axis, SWAP)


def in_order(own, other, place, axis):
    first = jnp.where(place == 0, own, other)
    second = jnp.where(place == 0, other, own)
    return jnp.stack([first, second], axis=axis)


def shifted(value, steps):
    count = lax.axis_size(FSDP)
    first, last = (max(0, -steps), min(count, count - steps))
    return lax.ppermute(value, FSDP, [(source, source + steps) for source in range(first, last)])


def summed_over_fsdp(value):
    count = lax.axis_size(FSDP)
    bit = 1
    while bit < count:
        value = value + lax.ppermute(value, FSDP, [(i, i ^ bit) for i in range(count)])
        bit *= 2
    return value


def line_gather(block):
    count, here = lax.axis_size(RING), lax.axis_index(RING)
    if count > LINE:
        return lax.all_gather(block, RING, axis=0)
    right, left = [block], [block]
    for step in range(1, count):
        right.append(
            lax.ppermute(right[-1], RING, [(i, i + 1) for i in range(step - 1, count - 1)])
        )
        left.append(
            lax.ppermute(left[-1], RING, [(i, i - 1) for i in range(1, count - step + 1)])
        )
    result = jnp.zeros((count,) + block.shape, block.dtype)
    for step in range(count):
        piece = block if step == 0 else jnp.where(here >= step, right[step], left[count - step])
        result = lax.dynamic_update_slice_in_dim(
            result, piece[None], (here - step + count) % count, axis=0
        )
    return result


def line_scatter(parts):
    count, here = lax.axis_size(RING), lax.axis_index(RING)
    if count > LINE:
        return wide(lax.psum_scatter(parts, RING, scatter_dimension=0, tiled=False))

    def part(place):
        return lax.dynamic_index_in_dim(parts, place, axis=0, keepdims=False)

    right, left = None, None
    for step in range(1, count):
        to_right, to_left = part(here + count - step), part(here - count + step)
        if step > 1:
            to_right = low(wide(to_right) + wide(right))
            to_left = low(wide(to_left) + wide(left))
        right = lax.ppermute(to_right, RING, [(i, i + 1) for i in range(step)])
        left = lax.ppermute(to_left, RING, [(i, i - 1) for i in range(count - step, count)])
    return wide(part(here)) + wide(right) + wide(left)


def gather_rows(shard):
    rows = line_gather(shard)
    rows = in_order(rows, swapped(rows, PAIR), lax.axis_index(PAIR), 1)
    rows = in_order(rows, swapped(rows, CORE), lax.axis_index(CORE), 2)
    return rows.reshape((-1,) + shard.shape[1:])


def scatter_rows(total):
    pair, core = lax.axis_index(PAIR), lax.axis_index(CORE)
    parts = low(total).reshape((lax.axis_size(RING), 2, 2, -1) + total.shape[1:])

    def halved(value, axis, place, name):
        mine = lax.dynamic_index_in_dim(value, place, axis=axis, keepdims=False)
        sent = lax.dynamic_index_in_dim(value, 1 - place, axis=axis, keepdims=False)
        return low(wide(mine) + wide(swapped(sent, name)))

    parts = halved(parts, 2, core, CORE)
    parts = halved(parts, 1, pair, PAIR)
    return line_scatter(parts)


def quarter_columns(shard):
    pair, core = lax.axis_index(PAIR), lax.axis_index(CORE)
    half = shard.shape[1] // 2

    def halved(value, place, width):
        mine = lax.dynamic_slice_in_dim(value, place * width, width, axis=value.ndim - 1)
        sent = lax.dynamic_slice_in_dim(value, (1 - place) * width, width, axis=value.ndim - 1)
        return mine, sent

    mine, sent = halved(shard, pair, half)
    rows = in_order(mine, swapped(sent, PAIR), pair, 0)
    mine, sent = halved(rows, core, half // 2)
    rows = in_order(mine, swapped(sent, CORE), core, 1)
    rows = line_gather(rows.reshape(-1, half // 2))
    return rows.reshape(-1, half // 2)


def quarter_to_owner(grad):
    pair, core = lax.axis_index(PAIR), lax.axis_index(CORE)
    width = grad.shape[1]
    block = lax.psum_scatter(
        grad.reshape(lax.axis_size(RING), -1, width), RING, scatter_dimension=0, tiled=False
    )
    block = block.reshape(2, 2, -1, width)

    def halved(value, axis, place):
        mine = lax.dynamic_index_in_dim(value, place, axis=axis, keepdims=False)
        sent = lax.dynamic_index_in_dim(value, 1 - place, axis=axis, keepdims=False)
        return mine, sent

    mine, sent = halved(block, 0, pair)
    block = in_order(mine, swapped(sent, PAIR), pair, 0)
    mine, sent = halved(block, 1, core)
    block = in_order(mine, swapped(sent, CORE), core, 1)
    return jnp.concatenate([wide(block[i, j]) for i in range(2) for j in range(2)], axis=1)


def four_blocks(value):
    over = swapped(value, PAIR)
    return jnp.concatenate([value, over, swapped(value, CORE), swapped(over, CORE)], axis=0)


def four_sums(total):
    half = total.shape[0] // 2
    total = total[:half] + wide(swapped(low(total[half:]), CORE))
    total = total[: half // 2] + wide(swapped(low(total[half // 2 :]), PAIR))
    return tensor_total(total)


def tensor_total(partial_sum):
    own = lax.reduce_precision(partial_sum, 8, 7)
    return own + wide(swapped(low(own), TENSOR))


def rotation(places, width):
    half_width = width // 2
    frequency = THETA ** (-(jnp.arange(half_width, dtype=jnp.float32) * 2.0) / width)
    angles = places.astype(jnp.float32)[:, None] * frequency[None, :]
    cosine = jnp.concatenate([jnp.cos(angles), jnp.cos(angles)], axis=-1)[:, None, :]
    sine_table = jnp.concatenate([jnp.sin(angles), jnp.sin(angles)], axis=-1)[:, None, :]
    return (cosine, sine_table)


def rotate(values, cosine, sine_table):
    half_width = values.shape[-1] // 2
    turned = jnp.concatenate([-values[..., half_width:], values[..., :half_width]], axis=-1)
    return values * cosine + turned * sine_table


def rotate_back(gradient, cosine, sine_table):
    half_width = gradient.shape[-1] // 2
    moved_part = gradient * sine_table
    return gradient * cosine + jnp.concatenate(
        [moved_part[..., half_width:], -moved_part[..., :half_width]], axis=-1
    )


def root_mean_square_parts(values):
    scale_row = lax.rsqrt(jnp.mean(values * values, axis=-1, keepdims=True) + EPSILON)
    return (values * scale_row, scale_row)


def norm_back(grad_normed, normalized, scale_row, gain):
    scaled = grad_normed * gain
    return scale_row * (scaled - normalized * jnp.mean(scaled * normalized, axis=-1, keepdims=True))


def visible(seg_row, pos_row, row_start, count_rows):
    pad_rows = BACK * count_rows
    seg_padded = jnp.concatenate([jnp.full((pad_rows,), -1, jnp.int32), seg_row])
    pos_padded = jnp.concatenate([jnp.zeros((pad_rows,), jnp.int32), pos_row])
    key_seg = lax.dynamic_slice_in_dim(seg_padded, row_start, pad_rows + count_rows)
    key_pos = lax.dynamic_slice_in_dim(pos_padded, row_start, pad_rows + count_rows)
    query_seg = lax.dynamic_slice_in_dim(seg_row, row_start, count_rows)
    query_pos = lax.dynamic_slice_in_dim(pos_row, row_start, count_rows)
    return (query_seg[:, None] == key_seg[None, :]) & (key_pos[None, :] <= query_pos[:, None])


def attend(query_rows, key_rows, value_rows, allowed):
    scores = jnp.einsum("thd,sd->hts", query_rows, key_rows, preferred_element_type=jnp.float32)
    scores = scores * (1.0 / math.sqrt(query_rows.shape[-1]))
    scores = jnp.where(allowed, scores, NEGATIVE)
    row_max = jnp.max(scores, axis=-1, keepdims=True)
    log_total = row_max + jnp.log(jnp.sum(jnp.exp(scores - row_max), axis=-1, keepdims=True))
    probs_low = low(jnp.exp(scores - log_total))
    mixed = jnp.einsum("hts,sd->thd", probs_low, value_rows, preferred_element_type=jnp.float32)
    return low(mixed.reshape(query_rows.shape[0], -1)), log_total


def log_total_of(query_rows, key_rows, allowed):
    scores = jnp.einsum("thd,sd->hts", query_rows, key_rows, preferred_element_type=jnp.float32)
    scores = scores * (1.0 / math.sqrt(query_rows.shape[-1]))
    scores = jnp.where(allowed, scores, NEGATIVE)
    row_max = jnp.max(scores, axis=-1, keepdims=True)
    return row_max + jnp.log(jnp.sum(jnp.exp(scores - row_max), axis=-1, keepdims=True))


def attend_back(grad_heads, query_rows, key_rows, value_rows, allowed, log_total):
    scale = 1.0 / math.sqrt(query_rows.shape[-1])
    scores = jnp.einsum("thd,sd->hts", query_rows, key_rows, preferred_element_type=jnp.float32)
    probs = jnp.exp(jnp.where(allowed, scores * scale, NEGATIVE) - log_total)
    grad_probs = jnp.einsum(
        "thd,sd->hts", grad_heads, value_rows, preferred_element_type=jnp.float32
    )
    row_inner = jnp.sum(probs * grad_probs, axis=-1, keepdims=True)
    grad_scores = low(probs * (grad_probs - row_inner))
    grad_query = jnp.einsum(
        "hts,sd->thd", grad_scores, key_rows, preferred_element_type=jnp.float32
    )
    grad_keys = jnp.einsum(
        "hts,thd->sd", grad_scores, query_rows, preferred_element_type=jnp.float32
    )
    grad_values = jnp.einsum(
        "hts,thd->sd", low(probs), grad_heads, preferred_element_type=jnp.float32
    )
    return grad_query * scale, grad_keys * scale, grad_values


def device(**coordinates):
    return {name: place for name, place in coordinates.items()}


class Copies:
    def __init__(self, send_sems, recv_sems):
        self.send_sems, self.recv_sems = send_sems, recv_sems
        self.used = 0
        self.sent = []

    def new(self):
        self.used += 1
        return self.used - 1

    def _make(self, which, source, target, to):
        return pltpu.make_async_remote_copy(
            src_ref=source,
            dst_ref=target,
            send_sem=self.send_sems.at[which],
            recv_sem=self.recv_sems.at[which],
            device_id=to,
            device_id_type=pl.DeviceIdType.MESH,
        )

    def send(self, which, source, target, to, cond=None):
        only(cond, lambda: self._make(which, source, target, to).start())
        self.sent.append((which, source, target, to, cond))

    def receive(self, which, target, via):
        self._make(which, target, target, via).wait_recv()

    def settle(self, until=None):
        until = len(self.sent) if until is None else until
        for i in range(until):
            if self.sent[i] is not None:
                which, source, target, to, cond = self.sent[i]
                only(cond, lambda: self._make(which, source, target, to).wait_send())
                self.sent[i] = None

    def left(self, which):
        for i, entry in enumerate(self.sent):
            if entry is not None and entry[0] == which:
                _, source, target, to, cond = entry
                only(cond, lambda: self._make(which, source, target, to).wait_send())
                self.sent[i] = None

    def settle_of(self, ids):
        for which in ids:
            self.left(which)

    def mark(self):
        return len(self.sent)


def only(cond, action):
    if cond is None:
        action()
    else:
        pl.when(cond)(action)


class Place:
    def __init__(self):
        self.z, self.p = lax.axis_index(RING), lax.axis_index(PAIR)
        self.c, self.y = lax.axis_index(CORE), lax.axis_index(TENSOR)
        self.q = self.p * 2 + self.c
        self.q_pair, self.q_core = (1 - self.p) * 2 + self.c, self.p * 2 + 1 - self.c
        self.q_cross = (1 - self.p) * 2 + 1 - self.c
        self.pair, self.core = {PAIR: 1 - self.p}, {CORE: 1 - self.c}
        self.cross = {PAIR: 1 - self.p, CORE: 1 - self.c}
        self.other = {TENSOR: 1 - self.y}
        self.near = {RING: self.z + 1 - 2 * (self.z % 2)}
        self.far = {RING: self.z + 2 - 4 * (self.z // 2)}
        self.right, self.left = {RING: self.z + 1}, {RING: self.z - 1}
        self.right_cross = {RING: self.z + 1, PAIR: 1 - self.p}
        self.left_cross = {RING: self.z - 1, PAIR: 1 - self.p}
        self.far_right = {RING: self.z + 2, PAIR: 0, CORE: 0}
        self.far_left = {RING: self.z - 2, PAIR: 1, CORE: 1}
        self.has_right, self.has_left = self.z < LINE - 1, self.z > 0
        self.has_far_right = (self.q == 3) & (self.z < LINE - 2)
        self.has_far_left = (self.q == 0) & (self.z > 1)

    def meet(self):
        barrier = pltpu.get_barrier_semaphore()

        def greet(to, cond=None):
            only(
                cond,
                lambda: pl.semaphore_signal(
                    barrier, inc=1, device_id=to, device_id_type=pl.DeviceIdType.MESH
                ),
            )

        for to in (self.pair, self.core, self.cross, self.other):
            greet(to)
        for far in (2, 3):
            greet({RING: self.z + far}, self.z + far < LINE)
            greet({RING: self.z - far}, self.z >= far)
        for there, to, cross in (
            (self.has_right, self.right, self.right_cross),
            (self.has_left, self.left, self.left_cross),
        ):
            greet(to, there)
            greet(cross, there)
        greet(self.far_right, self.has_far_right)
        greet(self.far_left, self.has_far_left)
        line = jnp.minimum(self.z, 1) + jnp.minimum(LINE - 1 - self.z, 1)
        upper = self.z // 2
        reach = self.p * self.c * (1 - upper) + (1 - self.p) * (1 - self.c) * upper
        pl.semaphore_wait(barrier, 4 + LINE - 1 + line + reach)


class LineFlow:
    def __init__(self, copies, place, block):
        self.copies, self.place, self.block = copies, place, block
        self.ids = {(way, step): copies.new() for way in (1, -1) for step in range(1, LINE)}

    def valid(self, way, step):
        z = self.place.z
        return z >= step if way == 1 else z + step <= LINE - 1

    def origin(self, way, step):
        return self.place.z - way * step

    def onward(self, way, step, source):
        if step == LINE - 1:
            return
        to = self.place.right if way == 1 else self.place.left
        there = self.place.has_right if way == 1 else self.place.has_left
        if step:
            there = there & self.valid(way, step)
        target = self.block(self.origin(way, step))
        self.copies.send(self.ids[way, step + 1], source, target, to, there)

    def start(self, source):
        self.onward(1, 0, source)
        self.onward(-1, 0, source)

    def arrive(self, step, then=None):
        for way in (1, -1):

            def take(way=way):
                target = self.block(self.origin(way, step))
                via = self.place.left if way == 1 else self.place.right
                self.copies.receive(self.ids[way, step], target, via)

            pl.when(self.valid(way, step))(take)
            if step < LINE - 1:
                self.onward(way, step, self.block(self.origin(way, step)))
            if then is not None:
                then(way, step)


class RowsFlow:
    def __init__(self, copies, place, shard, whole):
        self.copies, self.place, self.shard, self.whole = copies, place, shard, whole
        self.line = LineFlow(copies, place, lambda origin: self.rows(origin, place.p, place.c))
        items = [(0, 0)] + [(way, step) for step in range(1, LINE) for way in (1, -1)]
        self.items = items
        self.pair_ids = {item: copies.new() for item in items}
        self.core_ids = {item: copies.new() for item in items}
        self.cross_ids = {item: copies.new() for item in items}

    def rows(self, origin, p, c):
        count = self.shard.shape[0]
        return self.whole.at[pl.ds(pl.multiple_of((origin * 4 + p * 2 + c) * count, count), count)]

    def valid(self, item):
        return None if item == (0, 0) else self.line.valid(*item)

    def spread(self, way, step):
        item, place = (way, step), self.place
        here = self.rows(self.line.origin(way, step), place.p, place.c)
        self.copies.send(self.pair_ids[item], here, here, place.pair, self.valid(item))
        self.copies.send(self.core_ids[item], here, here, place.core, self.valid(item))

    def start(self, own_copy):
        self.line.start(self.shard)
        own_copy()
        self.spread(0, 0)

    def arrive(self, step):
        self.line.arrive(step, self.spread)

    def crossing(self, step):
        place = self.place
        for item in self.items:
            if item[1] != step:
                continue
            there = self.rows(self.line.origin(*item), 1 - place.p, place.c)
            only(
                self.valid(item),
                lambda: self.copies.receive(self.pair_ids[item], there, place.pair),
            )
            self.copies.send(self.cross_ids[item], there, there, place.core, self.valid(item))

    def end(self):
        place = self.place
        for item in self.items:
            origin = self.line.origin(*item)

            def take(item=item, origin=origin):
                mine = self.rows(origin, place.p, 1 - place.c)
                cross = self.rows(origin, 1 - place.p, 1 - place.c)
                self.copies.receive(self.core_ids[item], mine, place.core)
                self.copies.receive(self.cross_ids[item], cross, place.core)

            only(self.valid(item), take)


class QuarterFlow:
    def __init__(self, copies, place, shard, whole, columns, own_sem):
        self.copies, self.place, self.shard, self.whole = copies, place, shard, whole
        self.count, self.whole_width = shard.shape[0], shard.shape[1] // 4
        self.start_column, self.width = columns
        self.own = pltpu.make_async_copy(
            self.columns(place.p, place.c), self.rows(place.p, place.c), own_sem
        )
        self.near = (
            (copies.new(), 1 - place.p, place.c, place.pair),
            (copies.new(), place.p, 1 - place.c, place.core),
            (copies.new(), 1 - place.p, 1 - place.c, place.cross),
        )
        self.line = LineFlow(copies, place, self.block)

    def columns(self, p, c):
        start = (p * 2 + c) * self.whole_width + self.start_column
        return self.shard.at[:, pl.ds(pl.multiple_of(start, LANES), self.width)]

    def rows(self, p, c):
        count = self.count
        start = (self.place.z * 4 + p * 2 + c) * count
        return self.whole.at[pl.ds(pl.multiple_of(start, count), count)]

    def block(self, origin):
        count = 4 * self.count
        return self.whole.at[pl.ds(pl.multiple_of(origin * count, count), count)]

    def start(self):
        place = self.place
        self.own.start()
        for which, p, c, to in self.near:
            self.copies.send(which, self.columns(p, c), self.rows(place.p, place.c), to)

    def join(self):
        self.own.wait()
        for which, p, c, to in self.near:
            self.copies.receive(which, self.rows(p, c), to)
        self.line.start(self.block(self.place.z))

    def arrive(self, step):
        self.line.arrive(step)


class FourFlow:
    def __init__(self, copies, place, slots, parts):
        self.copies, self.place, self.slots = copies, place, slots
        self.rows = slots.shape[0] // 4
        self.size = self.rows // parts
        self.ids = [[copies.new() for _ in range(3)] for _ in range(parts)]

    def slot(self, which, part):
        return self.slots.at[pl.ds(which * self.rows + part * self.size, self.size)]

    def send(self, part, source):
        self.copies.send(self.ids[part][0], source, self.slot(1, part), self.place.pair)
        self.copies.send(self.ids[part][1], source, self.slot(2, part), self.place.core)

    def cross(self, part):
        got = self.slot(1, part)
        self.copies.receive(self.ids[part][0], got, self.place.pair)
        self.copies.send(self.ids[part][2], got, self.slot(3, part), self.place.core)

    def end(self, part):
        self.copies.receive(self.ids[part][1], self.slot(2, part), self.place.core)
        self.copies.receive(self.ids[part][2], self.slot(3, part), self.place.core)


def fetch(source, target, sem):
    copy = pltpu.make_async_copy(source, target, sem)
    copy.start()
    copy.wait()


def add_to(target, source):
    target[...] = low(wide(target[...]) + wide(source[...]))


class LineScatter:
    def __init__(self, copies, place, block, arrived, stage, sem):
        self.copies, self.place, self.block = copies, place, block
        self.arrived, self.stage, self.sem = arrived, stage, sem
        self.ids = {(way, step): copies.new() for way in (1, -1) for step in range(1, LINE)}

    def landing(self, way, step):
        return self.arrived.at[(1 - way) // 2, step - 1]

    def target(self, way, step):
        return self.block(self.place.z + way * (LINE - step))

    def takes(self, way, step):
        z = self.place.z
        if way == 1:
            return (z >= 1) & (z <= step)
        return (z <= LINE - 2) & (z >= LINE - 1 - step)

    def send(self, way, step, cond):
        to = self.place.right if way == 1 else self.place.left
        self.copies.send(
            self.ids[way, step], self.target(way, step), self.landing(way, step), to, cond
        )

    def start(self, ways=(1, -1)):
        for way in ways:
            for step in range(1, LINE):
                self.send(way, step, self.place.z == (0 if way == 1 else LINE - 1))

    def take(self, way, step):
        via = self.place.left if way == 1 else self.place.right
        self.copies.receive(self.ids[way, step], self.landing(way, step), via)
        fetch(self.landing(way, step), self.stage, self.sem)

    def step(self, step, ways=(1, -1)):
        for way in ways:
            there = self.takes(way, step - 1)

            def add(way=way):
                self.take(way, step - 1)
                add_to(self.target(way, step), self.stage)

            pl.when(there)(add)
            self.send(way, step, there)

    def finish(self, add):
        for way in (1, -1):

            def last(way=way):
                self.take(way, LINE - 1)
                add()

            pl.when(self.takes(way, LINE - 1))(last)


class QuarterScatter:
    def __init__(self, copies, place, grad, owner, columns, arrived, stage, sem, line=LineScatter):
        self.copies, self.place, self.grad, self.owner, self.sem = copies, place, grad, owner, sem
        self.stage = stage
        self.count, self.whole_width = owner.shape[0], owner.shape[1] // 4
        self.start_column, self.width = columns
        self.line = line(copies, place, self.block, arrived, stage, sem)
        self.near = (
            (copies.new(), 1 - place.p, place.c, place.pair),
            (copies.new(), place.p, 1 - place.c, place.core),
            (copies.new(), 1 - place.p, 1 - place.c, place.cross),
        )

    def block(self, origin):
        count = 4 * self.count
        return self.grad.at[pl.ds(pl.multiple_of(origin * count, count), count)]

    def rows(self, p, c):
        count = self.count
        start = (self.place.z * 4 + p * 2 + c) * count
        return self.grad.at[pl.ds(pl.multiple_of(start, count), count)]

    def columns(self, p, c):
        start = (p * 2 + c) * self.whole_width + self.start_column
        return self.owner.at[:, pl.ds(pl.multiple_of(start, LANES), self.width)]

    def finish(self):
        place = self.place
        self.line.finish(lambda: add_to(self.block(place.z), self.stage))
        for which, p, c, to in self.near:
            self.copies.send(which, self.rows(p, c), self.columns(place.p, place.c), to)
        fetch(self.rows(place.p, place.c), self.columns(place.p, place.c), self.sem)

    def end(self):
        for which, p, c, to in self.near:
            self.copies.receive(which, self.columns(p, c), to)


class ShortScatter:
    def __init__(self, copies, place, block, arrived, stage, sem):
        self.copies, self.place, self.block = copies, place, block
        self.arrived, self.stage, self.sem = arrived, stage, sem
        self.ids = {way: {name: copies.new() for name in "abcdef"} for way in (1, -1)}

    def at(self, way, k):
        return self.place.z == (k if way == 1 else LINE - 1 - k)

    def there(self, way, k):
        return k if way == 1 else LINE - 1 - k

    def landing(self, way, name):
        return self.arrived.at[(1 - way) // 2, 0 if name in "abc" else 1]

    def send(self, way, name, head, k, to):
        self.copies.send(
            self.ids[way][name],
            self.block(self.there(way, k)),
            self.landing(way, name),
            {RING: self.there(way, to)},
            self.at(way, head),
        )

    def take(self, way, name, source):
        landing = self.landing(way, name)
        self.copies.receive(self.ids[way][name], landing, {RING: self.there(way, source)})
        fetch(landing, self.stage, self.sem)

    def start(self, ways=(1, -1), names="abcd"):
        for name, head, k, to in (("a", 0, 2, 1), ("b", 1, 3, 2), ("c", 0, 3, 3), ("d", 0, 1, 1)):
            for way in ways:
                if name in names:
                    self.send(way, name, head, k, to)

    def step(self, ways=(1, -1)):
        for way in ways:
            for k, name, onward in ((1, "a", "e"), (2, "b", "f")):

                def add(way=way, k=k, name=name):
                    self.take(way, name, k - 1)
                    add_to(self.block(self.there(way, k + 1)), self.stage)

                pl.when(self.at(way, k))(add)
                self.send(way, onward, k, k + 1, k + 1)

    def finish(self, add):
        for way in (1, -1):
            for k, name, source in ((1, "d", 0), (2, "e", 1), (3, "c", 0), (3, "f", 2)):

                def last(way=way, name=name, source=source):
                    self.take(way, name, source)
                    add()

                pl.when(self.at(way, k))(last)


class DirectScatter:
    def __init__(self, copies, place, block, arrived, stage, sem):
        self.copies, self.place, self.block = copies, place, block
        self.arrived, self.stage, self.sem = arrived, stage, sem
        self.ids = {(way, far): copies.new() for way in (1, -1) for far in range(1, LINE)}

    def landing(self, way, far):
        return self.arrived.at[(1 - way) // 2, far - 1]

    def reaches(self, way, far):
        return self.place.z + far < LINE if way == 1 else self.place.z >= far

    def start(self):
        for far in range(LINE - 1, 0, -1):
            for way in (1, -1):
                there = self.place.z + way * far
                self.copies.send(
                    self.ids[way, far],
                    self.block(there),
                    self.landing(way, far),
                    {RING: there},
                    self.reaches(way, far),
                )

    def finish(self, add):
        for way in (1, -1):
            for far in range(1, LINE):

                def take(way=way, far=far):
                    via = {RING: self.place.z - way * far}
                    self.copies.receive(self.ids[way, far], self.landing(way, far), via)
                    fetch(self.landing(way, far), self.stage, self.sem)
                    add()

                pl.when(self.reaches(-way, far))(take)


class RowsScatter:
    def __init__(self, copies, place, whole, from_core, from_pair, arrived, stage, sem):
        self.copies, self.place, self.whole, self.sem = copies, place, whole, sem
        self.from_core, self.from_pair = from_core, from_pair
        self.count, self.columns = from_pair.shape[1], from_pair.shape[2]
        self.stage = stage
        self.core_id = copies.new()
        self.pair_ids = [copies.new() for _ in range(LINE)]
        self.line = DirectScatter(
            copies, place, lambda d: self.part(place.c, place.p, d), arrived, self.small(1), sem
        )

    def small(self, blocks):
        return self.stage.at[pl.ds(0, blocks * self.count), pl.ds(0, self.columns)]

    def part(self, c, p, origin, blocks=1):
        start = ((c * 2 + p) * LINE + origin) * self.count
        return self.whole.at[
            pl.ds(pl.multiple_of(start, self.count), blocks * self.count), pl.ds(0, self.columns)
        ]

    def fill(self, origin, value):
        for p in range(2):
            for c in range(2):
                start = (p * 2 + c) * self.count
                self.part(c, p, origin)[...] = value[start : start + self.count]

    def start(self):
        place = self.place
        self.copies.send(
            self.core_id, self.part(1 - place.c, 0, 0, 2 * LINE), self.from_core, place.core
        )

    def halve(self):
        place = self.place
        self.copies.receive(self.core_id, self.from_core, place.core)
        size = LINE * self.count
        for p in (1 - place.p, place.p):
            start = pl.multiple_of(p * size, size)
            fetch(self.from_core.at[pl.ds(start, size)], self.small(LINE), self.sem)
            add_to(self.part(place.c, p, 0, LINE), self.small(LINE))
            if p is place.p:
                continue
            for origin in (3, 0, 2, 1):
                self.copies.send(
                    self.pair_ids[origin],
                    self.part(place.c, p, origin),
                    self.from_pair.at[origin],
                    place.pair,
                )

    def quarter(self):
        place = self.place
        for origin in (3, 0, 2, 1):
            self.copies.receive(self.pair_ids[origin], self.from_pair.at[origin], place.pair)
            fetch(self.from_pair.at[origin], self.small(1), self.sem)
            add_to(self.part(place.c, place.p, origin), self.small(1))

    def finish(self, out):
        out[...] = wide(self.part(self.place.c, self.place.p, self.place.z)[...])

        def add():
            out[...] += wide(self.small(1)[...])

        self.line.finish(add)


PARTS = 4
NORMED_TILE = 768
BEFORE, NOW = 1, 5
N_REMOTE = 300
SUM_ROWS = 32


def eight_rows(value):
    return jnp.sum(value.reshape(-1, 8, value.shape[-1]), axis=0)


def layer_kernel(
    heads,
    head_size,
    tokens,
    first_shard,
    out_shard,
    gate_shard,
    up_shard,
    down_shard,
    grad_out,
    biases,
    cosine,
    sine,
    own_segments,
    own_positions,
    key_segments,
    key_positions,
    output,
    input_grad,
    grad_first,
    grad_w_out,
    grad_w_down,
    grad_w_gate,
    grad_w_up,
    sums_out,
    first_kept,
    normed_kept,
    line_landing,
    out_core_landing,
    out_pair_landing,
    out_other_landing,
    first_core_landing,
    first_pair_landing,
    first_line_landing,
    wo_core_landing,
    wo_pair_landing,
    wo_line_landing,
    first_all,
    w_out_all,
    state,
    window,
    keys,
    values,
    mail,
    query,
    heads_out,
    gate_all,
    up_all,
    down_all,
    normed_four,
    grad_four,
    hidden,
    grad_gate,
    grad_up,
    early_up,
    early_gate,
    pair_landing,
    other_landing,
    stage,
    grad_keys,
    grad_values,
    own_grad,
    window_landing,
    core_window,
    first_scale,
    second_scale,
    totals,
    sums,
    sums_landing,
    line_sums,
    send_sems,
    recv_sems,
    local_sems,
):
    place = Place()
    copies = Copies(send_sems, recv_sems)
    rows, width = tokens.shape
    batches = own_segments.shape[0]
    per_batch = rows // batches
    query_width = heads * head_size
    kv_width = query_width + 2 * head_size
    size = rows // PARTS
    root = 1.0 / math.sqrt(head_size)
    sem = local_sems.at[0]

    window[...] = jnp.zeros_like(window)
    place.meet()

    first = RowsFlow(copies, place, first_shard, first_all)
    outs = RowsFlow(copies, place, out_shard, w_out_all)
    quarter = gate_all.shape[1]
    first_half = -(-quarter // (2 * LANES)) * LANES
    halves = ((0, first_half), (first_half, quarter - first_half))

    def part_of(whole, half):
        return whole.at[:, pl.ds(*halves[half])]

    gates, ups, downs = [
        [
            QuarterFlow(
                copies, place, shard, part_of(whole, half), halves[half], local_sems.at[2 + i * 2 + half]
            )
            for half in range(2)
        ]
        for i, (shard, whole) in enumerate(
            ((gate_shard, gate_all), (up_shard, up_all), (down_shard, down_all))
        )
    ]
    cot = FourFlow(copies, place, grad_four, PARTS)
    second = FourFlow(copies, place, normed_four, PARTS)
    part_ids = [copies.new() for _ in range(PARTS)]
    window_ids = [copies.new() for _ in range(4)]
    window_core_ids = [copies.new() for _ in range(4)]

    def put(flow, sem):
        return lambda: fetch(flow.shard, flow.rows(place.z, place.p, place.c), sem)

    first.start(put(first, sem))
    gates[0].start()
    x = wide(tokens[...])
    first_scale[...] = lax.rsqrt(jnp.mean(x * x, axis=-1, keepdims=True) + EPSILON)
    state[...] = x * first_scale[...]
    outs.line.start(out_shard)
    first.crossing(0)
    first.arrive(1)
    outs.line.arrive(1)
    first.arrive(2)
    outs.line.arrive(2)
    first.arrive(3)
    ups[0].start()
    outs.line.arrive(3)
    gates[0].join()
    put(outs, sem)()
    for step in range(1, LINE):
        first.crossing(step)
    first.end()

    gains = wide(first_all[:, kv_width:]).T
    first_gain, second_gain = gains[0:1], gains[1:2]
    first_normed = mail.at[pl.ds(0, rows)]
    first_normed[...] = low(state[...] * first_gain)
    sign = jnp.where(
        lax.broadcasted_iota(jnp.int32, (1, head_size), 1) < head_size // 2, -1.0, 1.0
    )

    def project(start, size):
        raw = matmul(first_normed[...], first_all[:, start : start + size])
        return raw + biases[:, start : start + size]

    def turned(raw):
        half_turn = pltpu.roll(raw, head_size // 2, 1)
        return low(raw * cosine[...] + half_turn * (sine[...] * sign))

    def turned_back(gradient, mine):
        half_turn = pltpu.roll(gradient * sine[mine], head_size // 2, 1)
        return low(gradient * cosine[mine] - half_turn * sign)

    kv = project(query_width, 2 * head_size)
    key_now, value_now = turned(kv[:, :head_size]), low(kv[:, head_size:])
    for b in range(batches):
        mine = slice(b * per_batch, (b + 1) * per_batch)
        window[NOW + place.q, b, :, :head_size] = key_now[mine]
        window[NOW + place.q, b, :, head_size:] = value_now[mine]
    mine_now = window.at[NOW + place.q]
    copies.send(window_ids[0], mine_now, mine_now, place.pair)
    copies.send(window_core_ids[0], mine_now, mine_now, place.core)
    before = window.at[BEFORE + place.q]
    copies.send(window_ids[1], mine_now, before, place.right, place.has_right)
    copies.send(window_ids[2], mine_now, before, place.right_cross, place.has_right)
    copies.send(window_ids[3], mine_now, window.at[0], place.far_right, place.has_far_right)
    for h in range(0, heads, 2):
        raw = project(h * head_size, 2 * head_size)
        query[:, h * head_size : (h + 1) * head_size] = turned(raw[:, :head_size])
        query[:, (h + 1) * head_size : (h + 2) * head_size] = turned(raw[:, head_size:])
    keep_first = pltpu.make_async_copy(first_all, first_kept, local_sems.at[1])
    keep_first.start()
    for item in outs.items:
        outs.spread(*item)
    downs[0].start()
    ups[0].join()
    gates[0].arrive(1)
    copies.receive(window_ids[0], window.at[NOW + place.q_pair], place.pair)
    copies.send(
        window_core_ids[1],
        window.at[NOW + place.q_pair],
        window.at[NOW + place.q_pair],
        place.core,
    )

    def take_before():
        copies.receive(window_ids[1], window.at[BEFORE + place.q], place.left)
        copies.receive(window_ids[2], window.at[BEFORE + place.q_pair], place.left_cross)

    pl.when(place.has_left)(take_before)
    for i, at in ((2, BEFORE + place.q), (3, BEFORE + place.q_pair)):
        copies.send(window_core_ids[i], window.at[at], window.at[at], place.core, place.has_left)
    only(
        place.has_far_left,
        lambda: copies.receive(window_ids[3], window.at[0], place.far_left),
    )
    copies.receive(window_core_ids[0], window.at[NOW + place.q_core], place.core)
    copies.receive(window_core_ids[1], window.at[NOW + place.q_cross], place.core)

    def take_before_core():
        copies.receive(window_core_ids[2], window.at[BEFORE + place.q_core], place.core)
        copies.receive(window_core_ids[3], window.at[BEFORE + place.q_cross], place.core)

    pl.when(place.has_left)(take_before_core)
    cot_own = pltpu.make_async_copy(grad_out, grad_four.at[pl.ds(0, rows)], local_sems.at[8])
    cot_own.start()
    for i in range(PARTS):
        cot.send(i, grad_out.at[pl.ds(i * size, size)])

    def take_window(b):
        for slot in range(BACK + 1):
            at, there = place.q + slot, slice(slot * per_batch, (slot + 1) * per_batch)
            keys[there] = window[at, b, :, :head_size]
            values[there] = window[at, b, :, head_size:]

    def probabilities(b, mine, columns):
        scores = times_transpose(query[mine, columns], keys[...]) * root
        allowed = (own_segments[b] == key_segments[b]) & (key_positions[b] <= own_positions[b])
        scores = jnp.where(allowed, scores, NEGATIVE)
        weights = jnp.exp(scores - jnp.max(scores, axis=-1, keepdims=True))
        return weights * (1.0 / jnp.sum(weights, axis=-1, keepdims=True))

    part_own, part_other = mail.at[pl.ds(0, rows)], mail.at[pl.ds(rows, rows)]
    for b in range(batches):
        take_window(b)
        mine = slice(b * per_batch, (b + 1) * per_batch)

        def attend_head(h, carry, b=b, mine=mine):
            columns = pl.ds(pl.multiple_of(h * head_size, head_size), head_size)
            probs = low(probabilities(b, mine, columns))
            heads_out[mine, columns] = low(matmul(probs, values[...]))
            return carry

        lax.fori_loop(0, heads, attend_head, 0)
        if b == 0:
            for step in range(LINE):
                outs.crossing(step)
            outs.end()
            ups[0].arrive(1)
        part = low(times_transpose(heads_out[mine], w_out_all[...]))
        part_own[mine] = part
        for i in range(b * per_batch // size, (b + 1) * per_batch // size):
            block = pl.ds(i * size, size)
            copies.send(part_ids[i], part_own.at[block], part_other.at[block], place.other)
    early = copies.mark()

    for i in range(PARTS):
        block = pl.ds(i * size, size)
        copies.receive(part_ids[i], part_other.at[block], place.other)
        copies.left(part_ids[i])
        row_sum = wide(tokens[block]) + (wide(part_own[block]) + wide(part_other[block]))
        state[block] = row_sum
        scale_row = lax.rsqrt(jnp.mean(row_sum * row_sum, axis=-1, keepdims=True) + EPSILON)
        second_scale[block] = scale_row
        second.slot(0, i)[...] = low(row_sum * scale_row * second_gain)
        second.send(i, second.slot(0, i))
        if i == 0:
            gates[0].arrive(2)
            downs[0].join()
        if i == PARTS // 2:
            ups[0].arrive(2)
    downs[0].arrive(1)
    for flow in (gates[1], ups[1], downs[1]):
        flow.start()
    for part in range(PARTS):
        cot.cross(part)
        cot.end(part)
    for part in range(PARTS):
        second.cross(part)
    downs[0].arrive(2)
    keep_first.wait()
    for i in range(PARTS):
        second.end(i)
    gates[0].arrive(3)
    ups[0].arrive(3)

    tile = 256

    def forward_half(half):
        columns = pl.ds(*halves[half])

        def forward_tile(t, carry):
            block = pl.ds(pl.multiple_of(t * tile, tile), tile)
            gate = matmul(normed_four[block], gate_all[:, columns])
            up = matmul(normed_four[block], up_all[:, columns])
            sigmoid = 1.0 / (1.0 + jnp.exp(-gate))
            silu = gate * sigmoid
            hidden[block, columns] = low(silu * up)
            grad_up[block, columns] = low(silu)
            grad_gate[block, columns] = low(up * sigmoid * (1.0 + gate * (1.0 - sigmoid)))
            return carry

        lax.fori_loop(0, 4 * rows // tile, forward_tile, 0)

    def backward_half(half):
        columns = pl.ds(*halves[half])

        def backward_tile(t, carry):
            block = pl.ds(pl.multiple_of(t * tile, tile), tile)
            back = matmul(grad_four[block], down_all[:, columns])
            grad_gate[block, columns] = low(back * wide(grad_gate[block, columns]))
            grad_up[block, columns] = low(back * wide(grad_up[block, columns]))
            return carry

        lax.fori_loop(0, 4 * rows // tile, backward_tile, 0)

    def columns_of(d):
        return pl.ds(pl.multiple_of(d * rows, rows), rows)

    def weight_grad(target, left_side, right_side, half):
        columns = pl.ds(*halves[half])

        def block(d, carry):
            part = contract_rows(left_side[:, columns_of(d)], right_side[:, columns])
            target[columns_of(d)] = low(part)
            return carry

        lax.fori_loop(0, LINE, block, 0)

    grad_down = first_all
    down_backs, up_backs, gate_backs = [
        [
            QuarterScatter(
                copies,
                place,
                grads[half],
                owner,
                halves[half],
                line_landing.at[i * 2 + half, :, :, :, pl.ds(0, halves[half][1])],
                stage.at[:, pl.ds(0, halves[half][1])],
                sem,
                (LineScatter, ShortScatter)[half],
            )
            for half in range(2)
        ]
        for i, (grads, owner) in enumerate(
            (
                ([part_of(grad_down, 0), part_of(grad_down, 1)], grad_w_down),
                ([early_up, part_of(up_all, 1)], grad_w_up),
                ([early_gate, part_of(gate_all, 1)], grad_w_gate),
            )
        )
    ]

    forward_half(0)
    copies.settle(early)
    cot_own.wait()
    for flow in (gates[1], ups[1], downs[1]):
        flow.join()
    weight_grad(down_backs[0].grad, grad_four, hidden, 0)
    down_backs[0].line.start()
    downs[0].arrive(3)
    backward_half(0)
    weight_grad(up_backs[0].grad, normed_four, grad_up, 0)
    up_backs[0].line.start()
    weight_grad(gate_backs[0].grad, normed_four, grad_gate, 0)
    gate_backs[0].line.start()
    for flow in (gates[1], ups[1], downs[1]):
        flow.arrive(1)

    first_columns, later_columns = pl.ds(*halves[0]), pl.ds(*halves[1])
    step = halves[1][1]
    spares = (hidden, grad_gate, grad_up)[: width // step]
    for i, spare in enumerate(spares):

        def first_normed_tile(t, carry, i=i, spare=spare):
            block = columns_of(t)
            spare[block, later_columns] = low(
                times_transpose(grad_gate[block, first_columns], gate_all[i * step : (i + 1) * step, first_columns])
                + times_transpose(grad_up[block, first_columns], up_all[i * step : (i + 1) * step, first_columns])
            )
            return carry

        lax.fori_loop(0, 4, first_normed_tile, 0)
    keeps = [
        pltpu.make_async_copy(
            spare.at[:, later_columns],
            normed_kept.at[:, pl.ds(i * step, step)],
            local_sems.at[10 + i],
        )
        for i, spare in enumerate(spares)
    ]
    for keep in keeps:
        keep.start()
    down_backs[0].line.step(2)
    for flow in (gates[1], ups[1], downs[1]):
        flow.arrive(2)
    down_backs[0].line.step(3)
    for keep in keeps:
        keep.wait()
    gates[1].arrive(3)
    ups[1].arrive(3)

    forward_half(1)
    weight_grad(down_backs[1].grad, grad_four, hidden, 1)
    down_backs[1].line.start()
    up_backs[0].line.step(2)
    downs[1].arrive(3)
    backward_half(1)
    for flow in (cot, second):
        for ids in flow.ids:
            copies.settle_of(ids)
    for flow in (gates[1], ups[1]):
        copies.settle_of(flow.line.ids.values())

    normed_grad = grad_four
    core_ids = [copies.new() for _ in range(2)]
    pair_ids = [copies.new() for _ in range(PARTS)]
    other_ids = [copies.new() for _ in range(PARTS)]

    def slot(which, part=0, parts=1):
        return pl.ds(which * rows + part * (rows // parts), rows // parts)

    order = (3, 1, 2, 0)
    backs = [
        pltpu.make_async_copy(
            normed_kept.at[slot(which)], normed_grad.at[slot(which)], local_sems.at[10 + which]
        )
        for which in range(4)
    ]
    for which in order:
        backs[which].start()

    def normed_slot(which):
        backs[which].wait()

        def column_tile(t, carry):
            columns = pl.ds(pl.multiple_of(t * NORMED_TILE, NORMED_TILE), NORMED_TILE)
            normed_grad[slot(which), columns] = low(
                wide(normed_grad[slot(which), columns])
                + times_transpose(grad_gate[slot(which), later_columns], gate_all[columns, later_columns])
                + times_transpose(grad_up[slot(which), later_columns], up_all[columns, later_columns])
            )
            return carry

        lax.fori_loop(0, width // NORMED_TILE, column_tile, 0)

    def send_core(i):
        copies.send(
            core_ids[i], normed_grad.at[slot(2 + i)], mail.at[pl.ds(i * rows, rows)], place.core
        )

    normed_slot(3)
    send_core(1)
    normed_slot(1)
    copies.receive(core_ids[1], mail.at[pl.ds(rows, rows)], place.core)
    for i in range(PARTS):
        block = slot(1, i, PARTS)
        add_to(normed_grad.at[block], mail.at[pl.ds(rows + i * size, size)])
        copies.send(
            pair_ids[i],
            normed_grad.at[block],
            pair_landing.at[pl.ds(i * size, size)],
            place.pair,
        )
    normed_slot(2)
    send_core(0)
    normed_slot(0)
    copies.receive(core_ids[0], mail.at[pl.ds(0, rows)], place.core)
    add_to(normed_grad.at[slot(0)], mail.at[pl.ds(0, rows)])
    weight_grad(up_backs[1].grad, normed_four, grad_up, 1)
    up_backs[1].line.start((1,))
    up_backs[1].line.start((-1,), "b")
    down_backs[0].finish()
    up_backs[0].line.step(3)
    out_sum = normed_four
    out_core_id, out_pair_id, out_other_id = copies.new(), copies.new(), copies.new()
    first_weights = hidden
    first_fetch = pltpu.make_async_copy(first_kept, first_weights, local_sems.at[9])

    def out_tile(t, carry):
        block = columns_of(t)
        out_sum[block] = low(times_transpose(hidden[block], down_all[...]))
        return carry

    for i in range(PARTS):
        block = pl.ds(i * size, size)
        copies.receive(pair_ids[i], pair_landing.at[block], place.pair)
        add_to(normed_grad.at[block], pair_landing.at[block])
        copies.send(other_ids[i], normed_grad.at[block], other_landing.at[block], place.other)
        if i == 0:
            weight_grad(gate_backs[1].grad, normed_four, grad_gate, 1)
            gate_backs[1].line.start((1,))
            gate_backs[1].line.start((-1,), "b")
        if i == 1:
            lax.fori_loop(0, 4, out_tile, 0)
            copies.send(
                out_core_id, out_sum.at[pl.ds(2 * rows, 2 * rows)], out_core_landing, place.core
            )
            first_fetch.start()
        if i == 2:
            gate_backs[0].line.step(2)
    spare = mail.at[pl.ds(rows, rows)]
    copies.receive(out_core_id, out_core_landing, place.core)
    fetch(out_core_landing.at[pl.ds(rows, rows)], spare, sem)
    add_to(out_sum.at[slot(1)], spare)
    copies.send(out_pair_id, out_sum.at[slot(1)], out_pair_landing, place.pair)
    grad_own = mail.at[pl.ds(rows, rows)]
    grad_branch = mail.at[pl.ds(0, rows)]
    fetch(grad_out, grad_own, sem)
    second_sum = totals.at[:, pl.ds(kv_width, width)]
    second_sum[...] = jnp.zeros_like(second_sum)
    for i in range(PARTS):
        block = pl.ds(i * size, size)
        copies.receive(other_ids[i], other_landing.at[block], place.other)
        back = wide(normed_grad[block]) + wide(other_landing[block])
        scale_row = second_scale[block]
        unit = state[block] * scale_row
        second_sum[...] += eight_rows(back * unit)
        grad_state = wide(grad_own[block]) + norm_back(back, unit, scale_row, second_gain)
        input_grad[block] = grad_state
        grad_branch[block] = low(grad_state)

    grad_heads = grad_up.at[pl.ds(0, rows), pl.ds(0, query_width)]
    grad_raw = grad_up.at[pl.ds(rows, rows), pl.ds(0, kv_width)]
    grad_heads[...] = low(matmul(grad_branch[...], w_out_all[...]))
    back_ids = [copies.new() for _ in range(4)]
    back_core_ids = [copies.new() for _ in range(4)]
    for b in range(batches):
        take_window(b)
        mine = slice(b * per_batch, (b + 1) * per_batch)
        grad_keys[...] = jnp.zeros_like(grad_keys)
        grad_values[...] = jnp.zeros_like(grad_values)

        def attend_back_head(h, carry, b=b, mine=mine):
            columns = pl.ds(pl.multiple_of(h * head_size, head_size), head_size)
            probs = probabilities(b, mine, columns)
            grad_head = grad_heads[mine, columns]
            grad_probs = times_transpose(grad_head, values[...])
            row_inner = jnp.sum(probs * grad_probs, axis=-1, keepdims=True)
            grad_scores = low(probs * (grad_probs - row_inner))
            grad_raw[mine, columns] = turned_back(matmul(grad_scores, keys[...]) * root, mine)
            grad_keys[...] += contract_rows(grad_scores, query[mine, columns])
            grad_values[...] += contract_rows(low(probs), grad_head)
            return carry

        lax.fori_loop(0, heads, attend_back_head, 0)
        for at in range(NOW + 4):
            window[at, b] = jnp.zeros_like(window[at, b])
        for back in range(BACK + 1):
            at, there = place.q + back, slice(back * per_batch, (back + 1) * per_batch)
            window[at, b, :, :head_size] = low(grad_keys[there] * root)
            window[at, b, :, head_size:] = low(grad_values[there])
        own_grad[mine, :head_size] = grad_keys[there] * root
        own_grad[mine, head_size:] = grad_values[there]
    theirs = (NOW + place.q_core, NOW + place.q_cross, BEFORE + place.q_core, BEFORE + place.q_cross)
    ours = (NOW + place.q, NOW + place.q_pair, BEFORE + place.q, BEFORE + place.q_pair)
    for i in range(4):
        copies.send(back_core_ids[i], window.at[theirs[i]], core_window.at[i], place.core)
    copies.send(
        back_ids[3], window.at[0], window_landing.at[3], place.far_left, place.has_far_left
    )


    def add_own(landing):
        for b in range(batches):
            own_grad[b * per_batch : (b + 1) * per_batch] += wide(landing[b])

    for i in (1, 2, 3):
        copies.receive(back_core_ids[i], core_window.at[i], place.core)
        for b in range(batches):
            add_to(window.at[ours[i], b], core_window.at[i, b])
    copies.send(back_ids[0], window.at[ours[1]], window_landing.at[0], place.pair)
    copies.send(back_ids[1], window.at[ours[2]], window_landing.at[1], place.left, place.has_left)
    copies.send(
        back_ids[2], window.at[ours[3]], window_landing.at[2], place.left_cross, place.has_left
    )
    up_backs[0].finish()
    gate_backs[0].line.step(3)
    for name in "acd":
        up_backs[1].line.start((-1,), name)
        gate_backs[1].line.start((-1,), name)
    copies.receive(back_core_ids[0], core_window.at[0], place.core)
    add_own(core_window.at[0])
    wo_back = RowsScatter(
        copies, place, w_out_all, wo_core_landing, wo_pair_landing, wo_line_landing, stage, sem
    )
    for origin in range(LINE):
        branch = grad_branch[:, origin * rows : (origin + 1) * rows]
        wo_back.fill(origin, low(contract_rows(branch, heads_out[...])))
    wo_back.start()
    wo_back.halve()
    down_backs[1].line.step()
    up_backs[1].line.step((1,))
    fetch(out_core_landing.at[pl.ds(0, rows)], spare, sem)
    add_to(out_sum.at[slot(0)], spare)
    copies.receive(out_pair_id, out_pair_landing, place.pair)
    fetch(out_pair_landing, spare, sem)
    add_to(out_sum.at[slot(0)], spare)
    copies.send(out_other_id, out_sum.at[slot(0)], out_other_landing, place.other)
    copies.receive(back_ids[0], window_landing.at[0], place.pair)
    add_own(window_landing.at[0])

    def take_after():
        copies.receive(back_ids[1], window_landing.at[1], place.right)
        add_own(window_landing.at[1])
        copies.receive(back_ids[2], window_landing.at[2], place.right_cross)
        add_own(window_landing.at[2])

    pl.when(place.has_right)(take_after)

    def take_far():
        copies.receive(back_ids[3], window_landing.at[3], place.far_right)
        add_own(window_landing.at[3])

    pl.when(place.has_far_right)(take_far)
    every = slice(0, rows)
    grad_raw[:, query_width : query_width + head_size] = turned_back(
        own_grad[:, :head_size], every
    )
    grad_raw[:, query_width + head_size :] = low(own_grad[:, head_size:])
    first_back = RowsScatter(
        copies,
        place,
        grad_gate,
        first_core_landing,
        first_pair_landing,
        first_line_landing,
        stage,
        sem,
    )
    first_normed[...] = low(wide(tokens[...]) * first_scale[...] * first_gain)
    for origin in range(LINE):
        normed = first_normed[:, origin * rows : (origin + 1) * rows]
        first_back.fill(origin, low(contract_rows(normed, grad_raw[...])))
    first_back.start()

    first_ids = [copies.new() for _ in range(PARTS)]
    sum_ids = [copies.new() for _ in range(3)]
    first_at = kv_width + width
    first_own, first_other = mail.at[pl.ds(0, rows)], pair_landing
    first_fetch.wait()

    def first_tile(t, carry):
        block = pl.ds(pl.multiple_of(t * tile, tile), tile)
        part = times_transpose(grad_raw[...], first_weights[block, :kv_width])
        first_own[:, block] = low(part)
        unit = wide(tokens[:, block]) * first_scale[...]
        at = pl.ds(pl.multiple_of(first_at + t * tile, tile), tile)
        totals[:, at] = eight_rows(part * unit)
        return carry

    lax.fori_loop(0, width // tile, first_tile, 0)
    totals[:, :kv_width] = eight_rows(wide(grad_raw[...]))

    def sum_row(t, carry):
        columns = pl.ds(pl.multiple_of(t * LANES, LANES), LANES)
        sums[0, pl.ds(t, 1)] = jnp.sum(totals[:, columns], axis=0, keepdims=True)
        return carry

    lax.fori_loop(0, sums.shape[1], sum_row, 0)
    shared = first_at // LANES

    def sum_step(i, to):
        copies.send(sum_ids[i], sums.at[i], sums_landing.at[i], to)

    def sum_take(i, to):
        copies.receive(sum_ids[i], sums_landing.at[i], to)
        sums[i + 1] = sums[i]
        if i == 0:
            sums[1, shared:] += sums_landing[0, shared:]
        else:
            sums[i + 1] += sums_landing[i]

    def sum_line(way, far):
        return place.z + far < LINE if way == 1 else place.z >= far

    line_sum_ids = {(way, far): copies.new() for way in (1, -1) for far in range(1, LINE)}
    sum_step(0, place.other)
    for i in range(PARTS):
        block = pl.ds(i * size, size)
        copies.send(first_ids[i], first_own.at[block], first_other.at[block], place.other)
    first_back.halve()
    gate_backs[0].finish()
    gate_backs[1].line.step((1,))
    wo_back.quarter()
    wo_back.line.start()
    up_backs[1].line.step((-1,))
    first_back.quarter()
    gate_backs[1].line.step((-1,))
    first_back.line.start()
    sum_take(0, place.other)
    sum_step(1, place.pair)
    for i in range(PARTS):
        block = pl.ds(i * size, size)
        copies.receive(first_ids[i], first_other.at[block], place.other)
        unit = wide(tokens[block]) * first_scale[block]
        back = wide(first_own[block]) + wide(first_other[block])
        input_grad[block] += norm_back(back, unit, first_scale[block], first_gain)
    sum_take(1, place.pair)
    sum_step(2, place.core)
    sum_take(2, place.core)
    line_sums[place.z] = sums[3]
    for way in (1, -1):
        for far in range(1, LINE):
            copies.send(
                line_sum_ids[way, far],
                sums.at[3],
                line_sums.at[place.z],
                {RING: place.z + way * far},
                sum_line(way, far),
            )
    down_backs[1].finish()
    up_backs[1].finish()
    copies.receive(out_other_id, out_other_landing, place.other)
    fetch(out_other_landing, spare, sem)
    spare[...] = low(state[...] + (wide(out_sum[slot(0)]) + wide(spare[...])))
    fetch(spare, output, sem)
    gate_backs[1].finish()
    wo_back.finish(grad_w_out)
    first_back.finish(grad_first)
    for way in (1, -1):
        for far in range(1, LINE):
            source = place.z - way * far

            def take_sums(way=way, far=far, source=source):
                copies.receive(line_sum_ids[way, far], line_sums.at[source], {RING: source})

            pl.when(sum_line(-way, far))(take_sums)
    total = line_sums[0]
    for origin in range(1, LINE):
        total += line_sums[origin]
    sums_out[...] = total
    for scatter in down_backs + up_backs + gate_backs:
        scatter.end()
    copies.settle()


def layer_call(heads, head_size, operands):
    tokens, first_shard, out_shard, gate_shard = operands[:4]
    own_segments = operands[10]
    rows, width = tokens.shape
    batches = own_segments.shape[0]
    per_batch = rows // batches
    count, padded = gate_shard.shape
    quarter = padded // 4
    first_half = -(-quarter // (2 * LANES)) * LANES
    query_width = heads * head_size
    kv_width = query_width + 2 * head_size
    low_type, wide_type = jnp.bfloat16, jnp.float32
    in_vmem, anywhere = pl.BlockSpec(memory_space=pltpu.VMEM), pl.BlockSpec(memory_space=pl.ANY)

    def shape(*dims, kind=low_type):
        return jax.ShapeDtypeStruct(dims, kind)

    def vmem(*dims, kind=low_type):
        return pltpu.VMEM(dims, kind)

    sum_rows = (kv_width + 2 * width) // LANES
    outs = (
        (shape(rows, width), anywhere),
        (shape(rows, width, kind=wide_type), in_vmem),
        (shape(count, kv_width, kind=wide_type), in_vmem),
        (shape(count, query_width, kind=wide_type), in_vmem),
        (shape(count, padded), anywhere),
        (shape(count, padded), anywhere),
        (shape(count, padded), anywhere),
        (shape(sum_rows, LANES, kind=wide_type), in_vmem),
    )
    kept = (
        shape(width, first_shard.shape[1]),
        shape(4 * rows, width),
        shape(6, 2, LINE - 1, 4 * count, first_half),
        shape(2 * rows, width),
        shape(rows, width),
        shape(rows, width),
        shape(2 * LINE * count, kv_width),
        shape(LINE, count, kv_width),
        shape(2, LINE - 1, count, kv_width),
        shape(2 * LINE * count, query_width),
        shape(LINE, count, query_width),
        shape(2, LINE - 1, count, query_width),
    )
    scratch = (
        vmem(width, first_shard.shape[1]),
        vmem(width, query_width),
        vmem(rows, width, kind=wide_type),
        vmem(NOW + 4, batches, per_batch, 2 * head_size),
        vmem((BACK + 1) * per_batch, head_size),
        vmem((BACK + 1) * per_batch, head_size),
        vmem(2 * rows, width),
        vmem(rows, query_width),
        vmem(rows, query_width),
        vmem(width, quarter),
        vmem(width, quarter),
        vmem(width, quarter),
        vmem(4 * rows, width),
        vmem(4 * rows, width),
        vmem(4 * rows, quarter),
        vmem(4 * rows, quarter),
        vmem(4 * rows, quarter),
        vmem(width, first_half),
        vmem(width, first_half),
        vmem(rows, width),
        vmem(rows, width),
        vmem(4 * count, quarter),
        vmem((BACK + 1) * per_batch, head_size, kind=wide_type),
        vmem((BACK + 1) * per_batch, head_size, kind=wide_type),
        vmem(rows, 2 * head_size, kind=wide_type),
        vmem(4, batches, per_batch, 2 * head_size),
        vmem(4, batches, per_batch, 2 * head_size),
        vmem(rows, 1, kind=wide_type),
        vmem(rows, 1, kind=wide_type),
        vmem(8, sum_rows * LANES, kind=wide_type),
        vmem(4, sum_rows, LANES, kind=wide_type),
        vmem(3, sum_rows, LANES, kind=wide_type),
        vmem(LINE, sum_rows, LANES, kind=wide_type),
        pltpu.SemaphoreType.DMA((N_REMOTE,)),
        pltpu.SemaphoreType.DMA((N_REMOTE,)),
        pltpu.SemaphoreType.DMA((14,)),
    )
    results = pl.pallas_call(
        functools.partial(layer_kernel, heads, head_size),
        out_shape=[out[0] for out in outs] + list(kept),
        in_specs=[in_vmem] + [anywhere] * 6 + [in_vmem] * 7,
        out_specs=[out[1] for out in outs] + [anywhere] * len(kept),
        scratch_shapes=scratch,
        compiler_params=pltpu.CompilerParams(
            collective_id=0, has_side_effects=True, vmem_limit_bytes=VMEM_BYTES
        ),
    )(*operands)
    return results[: len(outs)]


def body(
    tokens,
    norm1_gain,
    query_weight,
    query_bias,
    key_weight,
    key_bias,
    value_weight,
    value_bias,
    output_weight,
    norm2_gain,
    gate_weight,
    up_weight,
    down_weight,
    cotangent,
    segments,
    positions,
):
    batches, count_rows, width = tokens.shape
    heads, head_size = query_bias.shape
    query_width = heads * head_size
    units = gate_weight.shape[1]
    place = lax.axis_index(FSDP)
    row_start = place * count_rows
    rows = batches * count_rows

    gains = jnp.stack([norm1_gain, norm2_gain], axis=1)
    gains = jnp.pad(gains, ((0, 0), (0, LANES - 2)))
    first_shard = jnp.concatenate([query_weight, key_weight, value_weight, gains], axis=1)
    kv_width = query_width + 2 * head_size
    padded = -(-units // (4 * LANES)) * (4 * LANES)

    def spaced(shard):
        return jnp.pad(shard, ((0, 0), (0, padded - units)))

    grad_out = cotangent.reshape(rows, width)
    inputs = wide(tokens.reshape(rows, width))
    biases = jnp.concatenate(
        [query_bias.reshape(-1), key_bias.reshape(-1), value_bias.reshape(-1)]
    )
    own_places = lax.dynamic_slice_in_dim(positions, row_start, count_rows, axis=1)
    cosine, sine_table = rotation(own_places.reshape(-1), head_size)
    if lax.axis_size(RING) == LINE:
        key_segments, key_positions = [], []
        for b in range(batches):
            padding = jnp.full((BACK * count_rows,), -1, jnp.int32)
            for rows_of, padded_rows in ((key_segments, segments), (key_positions, positions)):
                padded_rows = jnp.concatenate([padding, padded_rows[b]])
                rows_of.append(
                    lax.dynamic_slice_in_dim(padded_rows, row_start, (BACK + 1) * count_rows)
                )
        own_segments = lax.dynamic_slice_in_dim(segments, row_start, count_rows, axis=1)
        (
            output,
            input_grad,
            grad_w_qkv,
            grad_w_out,
            grad_w_down,
            grad_w_gate,
            grad_w_up,
            sums,
        ) = layer_call(
            heads,
            head_size,
            (
                tokens.reshape(rows, width),
                first_shard,
                output_weight.T,
                spaced(gate_weight),
                spaced(up_weight),
                spaced(down_weight.T),
                grad_out,
                wide(biases).reshape(1, -1),
                cosine[:, 0],
                sine_table[:, 0],
                own_segments[..., None],
                own_places[..., None],
                jnp.stack(key_segments)[:, None],
                jnp.stack(key_positions)[:, None],
            ),
        )
        sums = sums.reshape(-1)
        grad_w_down, grad_w_gate, grad_w_up = map(wide, (grad_w_down, grad_w_gate, grad_w_up))
    else:
        allowed = [
            visible(segments[b], positions[b], row_start, count_rows) for b in range(batches)
        ]
        first_all = gather_rows(first_shard)
        w_qkv = first_all[:, :kv_width]
        first_gain = wide(first_all[:, kv_width])
        second_gain = wide(first_all[:, kv_width + 1])
        w_out = gather_rows(output_weight.T)
        w_gate = quarter_columns(spaced(gate_weight))
        w_up = quarter_columns(spaced(up_weight))
        w_down = quarter_columns(spaced(down_weight.T))
        grad_out_four = four_blocks(grad_out)
        first_unit, first_scale = root_mean_square_parts(inputs)
        first_normed = low(first_unit * first_gain)
        raw = matmul(first_normed, w_qkv) + wide(biases)
        turned = rotate(
            raw[:, : query_width + head_size].reshape(rows, heads + 1, head_size),
            cosine,
            sine_table,
        )
        turned = low(turned)
        query_rows = turned[:, :heads].reshape(batches, count_rows, heads, head_size)
        key_value = jnp.concatenate(
            [turned[:, heads], low(raw[:, query_width + head_size :])], axis=1
        )
        key_value = key_value.reshape(batches, count_rows, 2 * head_size)
        window = jnp.concatenate(
            [shifted(key_value, back) for back in range(BACK, 0, -1)] + [key_value], axis=1
        )
        key_rows, value_rows = window[..., :head_size], window[..., head_size:]
        attended = [
            attend(query_rows[b], key_rows[b], value_rows[b], allowed[b]) for b in range(batches)
        ]
        log_totals = [log_total for _, log_total in attended]
        heads_out = jnp.concatenate([mixed for mixed, _ in attended], axis=0)
        residual = inputs + tensor_total(times_transpose(heads_out, w_out))
        second_unit, second_scale = root_mean_square_parts(residual)
        second_normed = four_blocks(low(second_unit * second_gain))

        second_unit, second_scale = root_mean_square_parts(residual)
        gate_value = matmul(second_normed, w_gate)
        up_part = matmul(second_normed, w_up)
        sigmoid_gate = jax.nn.sigmoid(gate_value)
        silu_gate = gate_value * sigmoid_gate
        hidden = low(silu_gate * up_part)
        grad_hidden = matmul(grad_out_four, w_down)
        grad_gate = low(
            grad_hidden * up_part * sigmoid_gate * (1.0 + gate_value * (1.0 - sigmoid_gate))
        )
        grad_up = low(grad_hidden * silu_gate)
        second_back = four_sums(times_transpose(grad_gate, w_gate) + times_transpose(grad_up, w_up))
        grad_w_down = quarter_to_owner(low(contract_rows(grad_out_four, hidden)))
        grad_w_gate = quarter_to_owner(low(contract_rows(second_normed, grad_gate)))
        grad_w_up = quarter_to_owner(low(contract_rows(second_normed, grad_up)))
        output = low(residual + four_sums(times_transpose(hidden, w_down)))

        second_gain_sum = jnp.sum(second_back * second_unit, axis=0)
        grad_state = wide(grad_out) + norm_back(second_back, second_unit, second_scale, second_gain)
        grad_branch = low(grad_state)
        grad_w_out = scatter_rows(contract_rows(grad_branch, heads_out))
        grad_heads = low(matmul(grad_branch, w_out)).reshape(query_rows.shape)
        backs = [
            attend_back(
                grad_heads[b], query_rows[b], key_rows[b], value_rows[b], allowed[b], log_totals[b]
            )
            for b in range(batches)
        ]
        grad_query = jnp.stack([back[0] for back in backs]).reshape(rows, heads, head_size)
        grad_window = jnp.stack([jnp.concatenate([back[1], back[2]], axis=1) for back in backs])
        own_grad = grad_window[:, BACK * count_rows :]
        for back in range(1, BACK + 1):
            first_row = (BACK - back) * count_rows
            own_grad = own_grad + wide(
                shifted(low(grad_window[:, first_row : first_row + count_rows]), -back)
            )
        own_grad = own_grad.reshape(rows, 2, head_size)
        turned_back = rotate_back(
            jnp.concatenate([grad_query, own_grad[:, :1]], axis=1), cosine, sine_table
        )
        grad_raw = low(jnp.concatenate([turned_back, own_grad[:, 1:]], axis=1).reshape(rows, -1))
        grad_w_qkv = scatter_rows(contract_rows(first_normed, grad_raw))
        bias_sum = jnp.sum(wide(grad_raw), axis=0)
        first_back_part = times_transpose(grad_raw, w_qkv)
        first_back = tensor_total(first_back_part)
        first_gain_sum = jnp.sum(first_back * first_unit, axis=0)
        input_grad = grad_state + norm_back(first_back, first_unit, first_scale, first_gain)
        sums = summed_over_fsdp(jnp.concatenate([bias_sum, second_gain_sum, first_gain_sum]))
    bias_total = sums[:kv_width]
    gain_rows = norm1_gain.shape[0]
    second_total = lax.dynamic_slice_in_dim(sums, kv_width + place * gain_rows, gain_rows)
    first_total = lax.dynamic_slice_in_dim(sums, kv_width + width + place * gain_rows, gain_rows)

    return (
        output.reshape(tokens.shape),
        input_grad.reshape(tokens.shape),
        first_total,
        grad_w_qkv[:, :query_width],
        bias_total[:query_width].reshape(query_bias.shape),
        grad_w_qkv[:, query_width : query_width + head_size],
        bias_total[query_width : query_width + head_size].reshape(key_bias.shape),
        grad_w_qkv[:, query_width + head_size :],
        bias_total[query_width + head_size :].reshape(value_bias.shape),
        grad_w_out.T,
        second_total,
        grad_w_gate[:, :units],
        grad_w_up[:, :units],
        grad_w_down[:, :units].T,
    )


def solution(mesh):
    fsdp, tensor = mesh.shape["fsdp"], mesh.shape["tensor"]
    fine = Mesh(mesh.devices.reshape(fsdp // 4, 2, 2, tensor), (RING, PAIR, CORE, TENSOR))
    by_rows, by_columns, by_tensor = P(FSDP, TENSOR), P(TENSOR, FSDP), P(TENSOR, None)
    by_tokens, by_gain = P(None, FSDP, None), P(FSDP)
    placed = (
        by_tokens,
        by_gain,
        by_rows,
        by_tensor,
        by_rows,
        by_tensor,
        by_rows,
        by_tensor,
        by_columns,
        by_gain,
        by_rows,
        by_rows,
        by_columns,
        by_tokens,
        P(),
        P(),
    )
    return jax.shard_map(
        body,
        mesh=fine,
        in_specs=placed,
        out_specs=(
            by_tokens,
            by_tokens,
            by_gain,
            by_rows,
            by_tensor,
            by_rows,
            by_tensor,
            by_rows,
            by_tensor,
            by_columns,
            by_gain,
            by_rows,
            by_rows,
            by_columns,
        ),
        check_vma=False,
    )
```

profile of v0, /device:TPU:0, one launch (start us, length us, event | category | flops | bytes accessed | tf_op | source)
XLA Modules:
  0.0 408.4 jit_solution(12010875812565244691)
XLA Ops:
  0.6 0.0 copy-start.2
  0.7 0.9 fusion.4
  1.5 0.1 pad_dynamic-slice_fusion.2
  1.6 0.6 broadcast_in_dim.16.key_segments
  2.2 0.8 fusion.3
  3.1 0.1 pad_dynamic-slice_fusion
  3.2 0.6 broadcast_in_dim.17.key_positions
  3.8 0.8 dynamic-slice_bitcast_fusion.1
  4.6 0.1 convert_element_type.31
  4.7 0.8 multiply_sine_fusion
  5.4 0.9 pad_maximum_fusion
  6.4 0.8 copy.38.own_positions
  7.2 0.8 dynamic-slice_bitcast_fusion
  7.9 0.8 copy.37.own_segments
  8.8 0.0 copy-done.2
  8.8 1.0 pad.19.gate_shard
  9.7 0.0 copy-done.3
  9.8 0.0 copy-start.10
  9.8 0.0 copy-start.11
  9.8 0.0 copy-start.12
  9.8 0.0 copy-start.13
  9.8 0.0 copy-start.14
  9.8 1.0 pad.20.up_shard
  10.8 0.0 copy-done.4
  10.8 1.0 pad.21.down_shard
  11.8 0.0 copy-done.15
  11.8 0.0 copy-done.16
  11.8 0.1 copy.36
  11.9 0.0 copy-done.9
  11.9 0.0 copy-done.10
  11.9 0.0 copy-done.11
  11.9 0.7 fusion.1.first_shard
  12.7 0.6 maximum_convert_fusion.biases
  13.3 381.2 %shard_map.263 = (bf16[384,1536]{1,0:T(8,128)(2,1)}, f32[384,1536]{1,0:T(8,128)}, f32[96,1024]{1,0:T(8,128)}, f32[96,768]{1,0:T(8,128)}, bf16[96,4608]{1,0:T(8,1...) custom-call(bf16[384,1536]{1,0:T(8,128)(2,1)} %bitcast.26, ...), custom_call_target="tpu_custom_call" | custom-call | tf_op jit(solution)/shard_map/pallas_call | solution.py:1642
  394.5 2.5 convert_bitcast_fusion
  397.0 0.0 copy-done.6
  397.0 1.3 slice_convert_fusion
  398.3 0.2 copy-done.5
  398.5 1.3 slice_convert_fusion.1
  399.8 0.7 slice.58
  400.5 0.6 fusion.2
  401.2 1.4 fusion.5
  402.5 1.3 slice.59
  403.8 1.3 fusion.6
  405.1 1.0 copy.45
  406.1 1.4 copy.46
  407.5 0.0 copy-done.8
  407.5 0.7 copy.47
  (26 shorter events, 0.1 us)
Async XLA Ops:
  0.6 8.1 %copy-start.2 = (bf16[96,4480]{1,0:T(8,128)(2,1)S(1)}, bf16[96,4480]{1,0:T(8,128)(2,1)}, u32[]{:S(2)}) copy-start(bf16[96,4480]{1,0:T(8,128)(2,1)} %param.26) | copy-start | bytes 2580484
  3.2 6.6 %copy-start.3 = (bf16[96,4480]{1,0:T(8,128)(2,1)S(1)}, bf16[96,4480]{1,0:T(8,128)(2,1)}, u32[]{:S(2)}) copy-start(bf16[96,4480]{1,0:T(8,128)(2,1)} %param.27) | copy-start | bytes 2580484
  8.8 2.0 copy-start.4
  9.8 2.0 copy-start.15
  9.8 2.0 copy-start.16
  9.8 2.2 copy-start.9
  9.8 2.2 copy-start.10
  9.8 2.2 copy-start.11
  9.8 2.9 copy-start.12
  9.8 2.9 copy-start.13
  9.8 2.8 copy-start.14
  394.4 2.6 copy-start.6
  397.0 1.5 copy-start.5
  398.3 1.5 copy-start.7
  398.3 6.8 %copy-start.1 = (bf16[384,1536]{1,0:T(8,128)(2,1)S(1)}, bf16[384,1536]{1,0:T(8,128)(2,1)}, u32[]{:S(2)}) copy-start(bf16[384,1536]{1,0:T(8,128)(2,1)} %get-tuple-element.22) | copy-start | bytes 3538948
  399.8 6.3 %copy-start = (f32[384,1536]{1,0:T(8,128)S(1)}, f32[384,1536]{1,0:T(8,128)}, u32[]{:S(2)}) copy-start(f32[384,1536]{1,0:T(8,128)} %get-tuple-element.23) | copy-start | bytes 7077892
  406.1 1.4 copy-start.8
where the time goes:
time: 414 us; the launch traced here: 408 us
  Pallas kernels  381 us (92%)
  local copies, waits for them, and re-layouts  17.3 us (4%)
  other arithmetic  8.93 us (2%)
    pallas_call x1, Pallas kernels, layer_call(): pl.pallas_call(functools.partial(layer_kernel, heads, head_size), out_sha...  381 us

commit v1 on v0

--- a/solution.py
+++ b/solution.py
@@ -12,7 +12,7 @@
 BACK = 5
 LINE = 4
 LANES = 128
-VMEM_BYTES = 63 * 1024 * 1024
+VMEM_BYTES = 65350 * 1024
 
 EPSILON = 1e-06
 THETA = 1000000.0
@@ -484,11 +484,10 @@
 class QuarterFlow:
     def __init__(self, copies, place, shard, whole, columns, own_sem):
         self.copies, self.place, self.shard, self.whole = copies, place, shard, whole
-        self.count, self.whole_width = shard.shape[0], shard.shape[1] // 4
+        self.count, self.quarter = shard.shape[0], -(-shard.shape[1] // (4 * LANES)) * LANES
         self.start_column, self.width = columns
-        self.own = pltpu.make_async_copy(
-            self.columns(place.p, place.c), self.rows(place.p, place.c), own_sem
-        )
+        self.last = min(self.width, shard.shape[1] - 3 * self.quarter - self.start_column)
+        self.own_sem = own_sem
         self.near = (
             (copies.new(), 1 - place.p, place.c, place.pair),
             (copies.new(), place.p, 1 - place.c, place.core),
@@ -496,29 +495,47 @@
         )
         self.line = LineFlow(copies, place, self.block)
 
-    def columns(self, p, c):
-        start = (p * 2 + c) * self.whole_width + self.start_column
-        return self.shard.at[:, pl.ds(pl.multiple_of(start, LANES), self.width)]
-
-    def rows(self, p, c):
-        count = self.count
-        start = (self.place.z * 4 + p * 2 + c) * count
-        return self.whole.at[pl.ds(pl.multiple_of(start, count), count)]
+    def columns(self, q, width):
+        start = q * self.quarter + self.start_column
+        return self.shard.at[:, pl.ds(pl.multiple_of(start, LANES), width)]
+
+    def rows(self, p, c, width):
+        start = (self.place.z * 4 + p * 2 + c) * self.count
+        rows = pl.ds(pl.multiple_of(start, self.count), self.count)
+        return self.whole.at[rows, pl.ds(0, width)]
 
     def block(self, origin):
         count = 4 * self.count
         return self.whole.at[pl.ds(pl.multiple_of(origin * count, count), count)]
 
+    def widths(self, q):
+        if self.last == self.width:
+            return ((None, self.width),)
+        return ((q == 3, self.last), (q != 3, self.width))
+
+    def own(self, width):
+        place = self.place
+        return pltpu.make_async_copy(
+            self.columns(place.q, width), self.rows(place.p, place.c, width), self.own_sem
+        )
+
     def start(self):
         place = self.place
-        self.own.start()
+        for cond, width in self.widths(place.q):
+            only(cond, lambda: self.own(width).start())
         for which, p, c, to in self.near:
-            self.copies.send(which, self.columns(p, c), self.rows(place.p, place.c), to)
+            for cond, width in self.widths(p * 2 + c):
+                target = self.rows(place.p, place.c, width)
+                self.copies.send(which, self.columns(p * 2 + c, width), target, to, cond)
 
     def join(self):
-        self.own.wait()
-        for which, p, c, to in self.near:
-            self.copies.receive(which, self.rows(p, c), to)
+        def take(width):
+            self.own(width).wait()
+            for which, p, c, to in self.near:
+                self.copies.receive(which, self.rows(p, c, width), to)
+
+        for cond, width in self.widths(self.place.q):
+            only(cond, lambda: take(width))
         self.line.start(self.block(self.place.z))
 
     def arrive(self, step):
@@ -804,11 +821,18 @@
             fetch(self.from_pair.at[origin], self.small(1), self.sem)
             add_to(self.part(place.c, place.p, origin), self.small(1))
 
-    def finish(self, out):
-        out[...] = wide(self.part(self.place.c, self.place.p, self.place.z)[...])
+    def finish(self, *outs):
+        start = 0
+        columns = []
+        for out in outs:
+            columns.append((out, slice(start, start + out.shape[1])))
+            start += out.shape[1]
+        for out, at in columns:
+            out[...] = wide(self.part(self.place.c, self.place.p, self.place.z)[:, at])
 
         def add():
-            out[...] += wide(self.small(1)[...])
+            for out, at in columns:
+                out[...] += wide(self.small(1)[:, at])
 
         self.line.finish(add)
 
@@ -818,6 +842,15 @@
 BEFORE, NOW = 1, 5
 N_REMOTE = 300
 SUM_ROWS = 32
+
+
+def clear_last(*wholes_and_shard):
+    *wholes, shard = wholes_and_shard
+    quarter = wholes[0].shape[1]
+    last = shard.shape[1] - 3 * quarter
+    if last < quarter:
+        for whole in wholes:
+            whole[:, last:] = jnp.zeros((whole.shape[0], quarter - last), whole.dtype)
 
 
 def eight_rows(value):
@@ -834,21 +867,26 @@
     up_shard,
     down_shard,
     grad_out,
-    biases,
+    query_bias,
+    key_bias,
+    value_bias,
     cosine,
     sine,
-    own_segments,
-    own_positions,
-    key_segments,
-    key_positions,
+    marks,
     output,
     input_grad,
-    grad_first,
+    grad_query_weight,
+    grad_key_weight,
+    grad_value_weight,
     grad_w_out,
     grad_w_down,
     grad_w_gate,
     grad_w_up,
-    sums_out,
+    query_bias_sum,
+    key_bias_sum,
+    value_bias_sum,
+    first_gain_out,
+    second_gain_out,
     first_kept,
     normed_kept,
     line_landing,
@@ -888,8 +926,8 @@
     own_grad,
     window_landing,
     core_window,
-    first_scale,
-    second_scale,
+    own_marks,
+    scales,
     totals,
     sums,
     sums_landing,
@@ -901,7 +939,7 @@
     place = Place()
     copies = Copies(send_sems, recv_sems)
     rows, width = tokens.shape
-    batches = own_segments.shape[0]
+    batches = marks.shape[0] // 4
     per_batch = rows // batches
     query_width = heads * head_size
     kv_width = query_width + 2 * head_size
@@ -910,6 +948,7 @@
     sem = local_sems.at[0]
 
     window[...] = jnp.zeros_like(window)
+    clear_last(gate_all, up_all, down_all, gate_shard)
     place.meet()
 
     first = RowsFlow(copies, place, first_shard, first_all)
@@ -944,8 +983,8 @@
     first.start(put(first, sem))
     gates[0].start()
     x = wide(tokens[...])
-    first_scale[...] = lax.rsqrt(jnp.mean(x * x, axis=-1, keepdims=True) + EPSILON)
-    state[...] = x * first_scale[...]
+    scales[:, 0:1] = lax.rsqrt(jnp.mean(x * x, axis=-1, keepdims=True) + EPSILON)
+    state[...] = x * scales[:, 0:1]
     outs.line.start(out_shard)
     first.crossing(0)
     first.arrive(1)
@@ -970,8 +1009,7 @@
     )
 
     def project(start, size):
-        raw = matmul(first_normed[...], first_all[:, start : start + size])
-        return raw + biases[:, start : start + size]
+        return matmul(first_normed[...], first_all[:, start : start + size])
 
     def turned(raw):
         half_turn = pltpu.roll(raw, head_size // 2, 1)
@@ -982,7 +1020,8 @@
         return low(gradient * cosine[mine] - half_turn * sign)
 
     kv = project(query_width, 2 * head_size)
-    key_now, value_now = turned(kv[:, :head_size]), low(kv[:, head_size:])
+    key_now = turned(kv[:, :head_size] + wide(key_bias[...]))
+    value_now = low(kv[:, head_size:] + wide(value_bias[...]))
     for b in range(batches):
         mine = slice(b * per_batch, (b + 1) * per_batch)
         window[NOW + place.q, b, :, :head_size] = key_now[mine]
@@ -996,8 +1035,9 @@
     copies.send(window_ids[3], mine_now, window.at[0], place.far_right, place.has_far_right)
     for h in range(0, heads, 2):
         raw = project(h * head_size, 2 * head_size)
-        query[:, h * head_size : (h + 1) * head_size] = turned(raw[:, :head_size])
-        query[:, (h + 1) * head_size : (h + 2) * head_size] = turned(raw[:, head_size:])
+        for i in range(2):
+            part = raw[:, i * head_size : (i + 1) * head_size] + wide(query_bias[h + i : h + i + 1])
+            query[:, (h + i) * head_size : (h + i + 1) * head_size] = turned(part)
     keep_first = pltpu.make_async_copy(first_all, first_kept, local_sems.at[1])
     keep_first.start()
     for item in outs.items:
@@ -1037,6 +1077,10 @@
     for i in range(PARTS):
         cot.send(i, grad_out.at[pl.ds(i * size, size)])
 
+    own_marks[...] = marks[:, marks.shape[1] - own_marks.shape[0] :].T
+    own_start = BACK * per_batch - (marks.shape[1] - own_marks.shape[0])
+    every_key = (BACK + 1) * per_batch
+
     def take_window(b):
         for slot in range(BACK + 1):
             at, there = place.q + slot, slice(slot * per_batch, (slot + 1) * per_batch)
@@ -1045,7 +1089,10 @@
 
     def probabilities(b, mine, columns):
         scores = times_transpose(query[mine, columns], keys[...]) * root
-        allowed = (own_segments[b] == key_segments[b]) & (key_positions[b] <= own_positions[b])
+        at = batches + b
+        own = own_marks[own_start : own_start + per_batch]
+        same = own[:, b : b + 1] == marks[b : b + 1, :every_key]
+        allowed = same & (marks[at : at + 1, :every_key] <= own[:, at : at + 1])
         scores = jnp.where(allowed, scores, NEGATIVE)
         weights = jnp.exp(scores - jnp.max(scores, axis=-1, keepdims=True))
         return weights * (1.0 / jnp.sum(weights, axis=-1, keepdims=True))
@@ -1081,7 +1128,7 @@
         row_sum = wide(tokens[block]) + (wide(part_own[block]) + wide(part_other[block]))
         state[block] = row_sum
         scale_row = lax.rsqrt(jnp.mean(row_sum * row_sum, axis=-1, keepdims=True) + EPSILON)
-        second_scale[block] = scale_row
+        scales[block, 1:2] = scale_row
         second.slot(0, i)[...] = low(row_sum * scale_row * second_gain)
         second.send(i, second.slot(0, i))
         if i == 0:
@@ -1334,7 +1381,7 @@
         block = pl.ds(i * size, size)
         copies.receive(other_ids[i], other_landing.at[block], place.other)
         back = wide(normed_grad[block]) + wide(other_landing[block])
-        scale_row = second_scale[block]
+        scale_row = scales[block, 1:2]
         unit = state[block] * scale_row
         second_sum[...] += eight_rows(back * unit)
         grad_state = wide(grad_own[block]) + norm_back(back, unit, scale_row, second_gain)
@@ -1418,6 +1465,18 @@
     fetch(out_pair_landing, spare, sem)
     add_to(out_sum.at[slot(0)], spare)
     copies.send(out_other_id, out_sum.at[slot(0)], out_other_landing, place.other)
+    first_at = kv_width + width
+    bias_rows = kv_width // LANES
+    gain_rows = first_shard.shape[0]
+    shared = bias_rows + width // gain_rows
+
+    def gain_sums(start, row):
+        for r in range(width // gain_rows):
+            part = totals[:, start + r * gain_rows : start + (r + 1) * gain_rows]
+            sums[0, row + r : row + r + 1, :gain_rows] = jnp.sum(part, axis=0, keepdims=True)
+
+    sums[0] = jnp.zeros_like(sums[0])
+    gain_sums(kv_width, bias_rows)
     copies.receive(back_ids[0], window_landing.at[0], place.pair)
     add_own(window_landing.at[0])
 
@@ -1449,7 +1508,7 @@
         stage,
         sem,
     )
-    first_normed[...] = low(wide(tokens[...]) * first_scale[...] * first_gain)
+    first_normed[...] = low(wide(tokens[...]) * scales[:, 0:1] * first_gain)
     for origin in range(LINE):
         normed = first_normed[:, origin * rows : (origin + 1) * rows]
         first_back.fill(origin, low(contract_rows(normed, grad_raw[...])))
@@ -1457,7 +1516,6 @@
 
     first_ids = [copies.new() for _ in range(PARTS)]
     sum_ids = [copies.new() for _ in range(3)]
-    first_at = kv_width + width
     first_own, first_other = mail.at[pl.ds(0, rows)], pair_landing
     first_fetch.wait()
 
@@ -1465,7 +1523,7 @@
         block = pl.ds(pl.multiple_of(t * tile, tile), tile)
         part = times_transpose(grad_raw[...], first_weights[block, :kv_width])
         first_own[:, block] = low(part)
-        unit = wide(tokens[:, block]) * first_scale[...]
+        unit = wide(tokens[:, block]) * scales[:, 0:1]
         at = pl.ds(pl.multiple_of(first_at + t * tile, tile), tile)
         totals[:, at] = eight_rows(part * unit)
         return carry
@@ -1478,8 +1536,8 @@
         sums[0, pl.ds(t, 1)] = jnp.sum(totals[:, columns], axis=0, keepdims=True)
         return carry
 
-    lax.fori_loop(0, sums.shape[1], sum_row, 0)
-    shared = first_at // LANES
+    lax.fori_loop(0, bias_rows, sum_row, 0)
+    gain_sums(first_at, shared)
 
     def sum_step(i, to):
         copies.send(sum_ids[i], sums.at[i], sums_landing.at[i], to)
@@ -1514,9 +1572,9 @@
     for i in range(PARTS):
         block = pl.ds(i * size, size)
         copies.receive(first_ids[i], first_other.at[block], place.other)
-        unit = wide(tokens[block]) * first_scale[block]
+        unit = wide(tokens[block]) * scales[block, 0:1]
         back = wide(first_own[block]) + wide(first_other[block])
-        input_grad[block] += norm_back(back, unit, first_scale[block], first_gain)
+        input_grad[block] += norm_back(back, unit, scales[block, 0:1], first_gain)
     sum_take(1, place.pair)
     sum_step(2, place.core)
     sum_take(2, place.core)
@@ -1538,7 +1596,7 @@
     fetch(spare, output, sem)
     gate_backs[1].finish()
     wo_back.finish(grad_w_out)
-    first_back.finish(grad_first)
+    first_back.finish(grad_query_weight, grad_key_weight, grad_value_weight)
     for way in (1, -1):
         for far in range(1, LINE):
             source = place.z - way * far
@@ -1550,7 +1608,12 @@
     total = line_sums[0]
     for origin in range(1, LINE):
         total += line_sums[origin]
-    sums_out[...] = total
+    sums_landing[0] = total
+    query_bias_sum[...] = sums_landing[0, :heads]
+    key_bias_sum[...] = sums_landing[0, heads : heads + 1]
+    value_bias_sum[...] = sums_landing[0, heads + 1 : heads + 2]
+    second_gain_out[...] = sums_landing[0, pl.ds(bias_rows + place.z * 4 + place.q, 1)]
+    first_gain_out[...] = sums_landing[0, pl.ds(shared + place.z * 4 + place.q, 1)]
     for scatter in down_backs + up_backs + gate_backs:
         scatter.end()
     copies.settle()
@@ -1558,11 +1621,12 @@
 
 def layer_call(heads, head_size, operands):
     tokens, first_shard, out_shard, gate_shard = operands[:4]
-    own_segments = operands[10]
+    marks = operands[-1]
     rows, width = tokens.shape
-    batches = own_segments.shape[0]
+    batches = marks.shape[0] // 4
     per_batch = rows // batches
-    count, padded = gate_shard.shape
+    count, units = gate_shard.shape
+    padded = -(-units // (4 * LANES)) * (4 * LANES)
     quarter = padded // 4
     first_half = -(-quarter // (2 * LANES)) * LANES
     query_width = heads * head_size
@@ -1576,16 +1640,24 @@
     def vmem(*dims, kind=low_type):
         return pltpu.VMEM(dims, kind)
 
-    sum_rows = (kv_width + 2 * width) // LANES
+    sum_rows = kv_width // LANES + 2 * (width // count)
+    total_columns = kv_width + 2 * width
+    own_rows = marks.shape[1] - BACK * per_batch // LANES * LANES
     outs = (
         (shape(rows, width), anywhere),
         (shape(rows, width, kind=wide_type), in_vmem),
-        (shape(count, kv_width, kind=wide_type), in_vmem),
+        (shape(count, query_width, kind=wide_type), in_vmem),
+        (shape(count, head_size, kind=wide_type), in_vmem),
+        (shape(count, head_size, kind=wide_type), in_vmem),
         (shape(count, query_width, kind=wide_type), in_vmem),
         (shape(count, padded), anywhere),
         (shape(count, padded), anywhere),
         (shape(count, padded), anywhere),
-        (shape(sum_rows, LANES, kind=wide_type), in_vmem),
+        (shape(heads, head_size, kind=wide_type), in_vmem),
+        (shape(1, head_size, kind=wide_type), in_vmem),
+        (shape(1, head_size, kind=wide_type), in_vmem),
+        (shape(1, LANES, kind=wide_type), in_vmem),
+        (shape(1, LANES, kind=wide_type), in_vmem),
     )
     kept = (
         shape(width, first_shard.shape[1]),
@@ -1623,15 +1695,15 @@
         vmem(width, first_half),
         vmem(rows, width),
         vmem(rows, width),
-        vmem(4 * count, quarter),
+        vmem(4 * count, max(kv_width, first_half)),
         vmem((BACK + 1) * per_batch, head_size, kind=wide_type),
         vmem((BACK + 1) * per_batch, head_size, kind=wide_type),
         vmem(rows, 2 * head_size, kind=wide_type),
         vmem(4, batches, per_batch, 2 * head_size),
         vmem(4, batches, per_batch, 2 * head_size),
-        vmem(rows, 1, kind=wide_type),
-        vmem(rows, 1, kind=wide_type),
-        vmem(8, sum_rows * LANES, kind=wide_type),
+        vmem(own_rows, marks.shape[0], kind=wide_type),
+        vmem(rows, 2, kind=wide_type),
+        vmem(8, total_columns, kind=wide_type),
         vmem(4, sum_rows, LANES, kind=wide_type),
         vmem(3, sum_rows, LANES, kind=wide_type),
         vmem(LINE, sum_rows, LANES, kind=wide_type),
@@ -1642,7 +1714,7 @@
     results = pl.pallas_call(
         functools.partial(layer_kernel, heads, head_size),
         out_shape=[out[0] for out in outs] + list(kept),
-        in_specs=[in_vmem] + [anywhere] * 6 + [in_vmem] * 7,
+        in_specs=[in_vmem] + [anywhere] * 6 + [in_vmem] * 6,
         out_specs=[out[1] for out in outs] + [anywhere] * len(kept),
         scratch_shapes=scratch,
         compiler_params=pltpu.CompilerParams(
@@ -1650,6 +1722,29 @@
         ),
     )(*operands)
     return results[: len(outs)]
+
+
+def results_kernel(*refs):
+    count = len(refs) // 2
+    for source, target in zip(refs[:count], refs[count:]):
+        if len(target.shape) == 1:
+            target[...] = source[0, : target.shape[0]]
+        else:
+            target[...] = source[:, : target.shape[1]].astype(target.dtype)
+
+
+def results_call(as_they_are, widened, units, vectors, vector_size):
+    shapes = [jax.ShapeDtypeStruct(value.shape, value.dtype) for value in as_they_are]
+    shapes += [jax.ShapeDtypeStruct((value.shape[0], units), jnp.float32) for value in widened]
+    shapes += [jax.ShapeDtypeStruct((vector_size,), jnp.float32) for _ in vectors]
+    in_vmem = pl.BlockSpec(memory_space=pltpu.VMEM)
+    return pl.pallas_call(
+        results_kernel,
+        out_shape=shapes,
+        in_specs=[in_vmem] * len(shapes),
+        out_specs=[in_vmem] * len(shapes),
+        compiler_params=pltpu.CompilerParams(vmem_limit_bytes=VMEM_BYTES),
+    )(*as_they_are, *widened, *vectors)
 
 
 def body(
@@ -1695,24 +1790,29 @@
     own_places = lax.dynamic_slice_in_dim(positions, row_start, count_rows, axis=1)
     cosine, sine_table = rotation(own_places.reshape(-1), head_size)
     if lax.axis_size(RING) == LINE:
-        key_segments, key_positions = [], []
-        for b in range(batches):
-            padding = jnp.full((BACK * count_rows,), -1, jnp.int32)
-            for rows_of, padded_rows in ((key_segments, segments), (key_positions, positions)):
-                padded_rows = jnp.concatenate([padding, padded_rows[b]])
-                rows_of.append(
-                    lax.dynamic_slice_in_dim(padded_rows, row_start, (BACK + 1) * count_rows)
-                )
-        own_segments = lax.dynamic_slice_in_dim(segments, row_start, count_rows, axis=1)
+        marks = jnp.concatenate([segments, positions]).astype(jnp.float32)
+        lanes = -(-(BACK + 1) * count_rows // LANES) * LANES
+        marks = jnp.pad(
+            marks,
+            ((0, 2 * batches), (BACK * count_rows, lanes - (BACK + 1) * count_rows)),
+            constant_values=-1.0,
+        )
+        marks = lax.dynamic_slice_in_dim(marks, row_start, lanes, axis=1)
         (
             output,
             input_grad,
-            grad_w_qkv,
+            grad_query_weight,
+            grad_key_weight,
+            grad_value_weight,
             grad_w_out,
             grad_w_down,
             grad_w_gate,
             grad_w_up,
-            sums,
+            query_bias_sum,
+            key_bias_sum,
+            value_bias_sum,
+            first_gain_sum,
+            second_gain_sum,
         ) = layer_call(
             heads,
             head_size,
@@ -1720,21 +1820,50 @@
                 tokens.reshape(rows, width),
                 first_shard,
                 output_weight.T,
-                spaced(gate_weight),
-                spaced(up_weight),
-                spaced(down_weight.T),
+                gate_weight,
+                up_weight,
+                down_weight.T,
                 grad_out,
-                wide(biases).reshape(1, -1),
+                query_bias,
+                key_bias,
+                value_bias,
                 cosine[:, 0],
                 sine_table[:, 0],
-                own_segments[..., None],
-                own_places[..., None],
-                jnp.stack(key_segments)[:, None],
-                jnp.stack(key_positions)[:, None],
+                marks,
             ),
         )
-        sums = sums.reshape(-1)
-        grad_w_down, grad_w_gate, grad_w_up = map(wide, (grad_w_down, grad_w_gate, grad_w_up))
+        (
+            output,
+            input_grad,
+            grad_query_weight,
+            grad_key_weight,
+            grad_value_weight,
+            grad_w_out,
+            query_bias_sum,
+            key_bias_sum,
+            value_bias_sum,
+            grad_w_down,
+            grad_w_gate,
+            grad_w_up,
+            first_total,
+            second_total,
+        ) = results_call(
+            (
+                output,
+                input_grad,
+                grad_query_weight,
+                grad_key_weight,
+                grad_value_weight,
+                grad_w_out,
+                query_bias_sum,
+                key_bias_sum,
+                value_bias_sum,
+            ),
+            (grad_w_down, grad_w_gate, grad_w_up),
+            units,
+            (first_gain_sum, second_gain_sum),
+            norm1_gain.shape[0],
+        )
     else:
         allowed = [
             visible(segments[b], positions[b], row_start, count_rows) for b in range(batches)
@@ -1823,21 +1952,27 @@
         first_gain_sum = jnp.sum(first_back * first_unit, axis=0)
         input_grad = grad_state + norm_back(first_back, first_unit, first_scale, first_gain)
         sums = summed_over_fsdp(jnp.concatenate([bias_sum, second_gain_sum, first_gain_sum]))
-    bias_total = sums[:kv_width]
-    gain_rows = norm1_gain.shape[0]
-    second_total = lax.dynamic_slice_in_dim(sums, kv_width + place * gain_rows, gain_rows)
-    first_total = lax.dynamic_slice_in_dim(sums, kv_width + width + place * gain_rows, gain_rows)
+        bias_total = sums[:kv_width]
+        gain_rows = norm1_gain.shape[0]
+        second_total = lax.dynamic_slice_in_dim(sums, kv_width + place * gain_rows, gain_rows)
+        first_total = lax.dynamic_slice_in_dim(sums, kv_width + width + place * gain_rows, gain_rows)
+        grad_query_weight = grad_w_qkv[:, :query_width]
+        grad_key_weight = grad_w_qkv[:, query_width : query_width + head_size]
+        grad_value_weight = grad_w_qkv[:, query_width + head_size :]
+        query_bias_sum = bias_total[:query_width].reshape(query_bias.shape)
+        key_bias_sum = bias_total[query_width : query_width + head_size].reshape(key_bias.shape)
+        value_bias_sum = bias_total[query_width + head_size :].reshape(value_bias.shape)
 
     return (
         output.reshape(tokens.shape),
         input_grad.reshape(tokens.shape),
         first_total,
-        grad_w_qkv[:, :query_width],
-        bias_total[:query_width].reshape(query_bias.shape),
-        grad_w_qkv[:, query_width : query_width + head_size],
-        bias_total[query_width : query_width + head_size].reshape(key_bias.shape),
-        grad_w_qkv[:, query_width + head_size :],
-        bias_total[query_width + head_size :].reshape(value_bias.shape),
+        grad_query_weight,
+        query_bias_sum,
+        grad_key_weight,
+        key_bias_sum,
+        grad_value_weight,
+        value_bias_sum,
         grad_w_out.T,
         second_total,
         grad_w_gate[:, :units],

time: 414 us -> 401 us (0.969)
  local copies, waits for them, and re-layouts: 17.3 us -> 0.92 us
  Pallas kernels: 381 us -> 388 us
    pallas_call x0 -> x1, Pallas kernels: none -> 6.8 us  [results_call(): pl.pallas_call(results_kernel, out_shape=shapes, in_specs=[in_vmem] * len...]
    slice x6 -> x0, local copies, waits for them, and re-layouts: 5.6 us -> none  [the longest x2 1.69 us: body(): padded_rows = jnp.concatenate([padding, padded_rows[b]])]
where the time goes in v1:
time: 401 us; the launch traced here: 396 us
  Pallas kernels  388 us (97%)
  other arithmetic  5.56 us (1%)
    pallas_call x1, Pallas kernels, layer_call(): pl.pallas_call(functools.partial(layer_kernel, heads, head_size), out_sha...  382 us

profile of v1, /device:TPU:0, one launch (start us, length us, event | category | flops | bytes accessed | tf_op | source)
XLA Modules:
  0.0 395.8 jit_solution(5438875021326219569)
XLA Ops:
  0.7 0.7 pad_maximum_fusion.2
  1.3 0.8 dynamic-slice_convert_fusion
  2.1 0.1 convert_element_type.16
  2.2 0.1 copy.32
  2.3 0.8 add_convert_fusion
  3.1 0.7 pad_dynamic-slice_fusion.marks
  3.8 1.6 fusion.1.first_shard
  5.5 0.8 multiply_sine_fusion
  6.2 0.9 pad_maximum_fusion
  7.1 381.7 %shard_map.263 = (bf16[384,1536]{1,0:T(8,128)(2,1)}, f32[384,1536]{1,0:T(8,128)}, f32[96,768]{1,0:T(8,128)}, f32[96,128]{1,0:T(8,128)}, f32[96,128]{1,0:T(8,128)...) custom-call(bf16[384,1536]{1,0:T(8,128)(2,1)} %bitcast.10, ...), custom_call_target="tpu_custom_call" | custom-call | tf_op jit(solution)/shard_map/pallas_call | solution.py:1714
  388.8 6.8 %shard_map.264 = (bf16[384,1536]{1,0:T(8,128)(2,1)}, f32[384,1536]{1,0:T(8,128)}, f32[96,768]{1,0:T(8,128)}, f32[96,128]{1,0:T(8,128)}, f32[96,128]{1,0:T(8,128)...) custom-call(bf16[384,1536]{1,0:T(8,128)(2,1)} %get-tuple-element.42., ...), custom_call_target="tpu_custom_call" | custom-call | tf_op jit(solution)/shard_map/pallas_call | solution.py:1741
  (1 shorter events, 0.0 us)

commit v2 on v1

--- a/solution.py
+++ b/solution.py
@@ -3,6 +3,7 @@
 
 import jax
 import jax.numpy as jnp
+import numpy as np
 from jax import lax
 from jax.experimental import pallas as pl
 from jax.experimental.pallas import tpu as pltpu
@@ -840,7 +841,7 @@
 PARTS = 4
 NORMED_TILE = 768
 BEFORE, NOW = 1, 5
-N_REMOTE = 300
+N_REMOTE = 360
 SUM_ROWS = 32
 
 
@@ -870,8 +871,7 @@
     query_bias,
     key_bias,
     value_bias,
-    cosine,
-    sine,
+    frequency,
     marks,
     output,
     input_grad,
@@ -927,6 +927,8 @@
     window_landing,
     core_window,
     own_marks,
+    cosine,
+    sine,
     scales,
     totals,
     sums,
@@ -986,6 +988,14 @@
     scales[:, 0:1] = lax.rsqrt(jnp.mean(x * x, axis=-1, keepdims=True) + EPSILON)
     state[...] = x * scales[:, 0:1]
     outs.line.start(out_shard)
+    own_marks[...] = marks[:, marks.shape[1] - own_marks.shape[0] :].T
+    own_start = BACK * per_batch - (marks.shape[1] - own_marks.shape[0])
+    every_key = (BACK + 1) * per_batch
+    for b in range(batches):
+        places = own_marks[own_start : own_start + per_batch, batches + b : batches + b + 1]
+        angles = places * frequency[...]
+        cosine[b * per_batch : (b + 1) * per_batch] = jnp.cos(angles)
+        sine[b * per_batch : (b + 1) * per_batch] = jnp.sin(angles)
     first.crossing(0)
     first.arrive(1)
     outs.line.arrive(1)
@@ -1077,9 +1087,6 @@
     for i in range(PARTS):
         cot.send(i, grad_out.at[pl.ds(i * size, size)])
 
-    own_marks[...] = marks[:, marks.shape[1] - own_marks.shape[0] :].T
-    own_start = BACK * per_batch - (marks.shape[1] - own_marks.shape[0])
-    every_key = (BACK + 1) * per_batch
 
     def take_window(b):
         for slot in range(BACK + 1):
@@ -1459,12 +1466,6 @@
     wo_back.halve()
     down_backs[1].line.step()
     up_backs[1].line.step((1,))
-    fetch(out_core_landing.at[pl.ds(0, rows)], spare, sem)
-    add_to(out_sum.at[slot(0)], spare)
-    copies.receive(out_pair_id, out_pair_landing, place.pair)
-    fetch(out_pair_landing, spare, sem)
-    add_to(out_sum.at[slot(0)], spare)
-    copies.send(out_other_id, out_sum.at[slot(0)], out_other_landing, place.other)
     first_at = kv_width + width
     bias_rows = kv_width // LANES
     gain_rows = first_shard.shape[0]
@@ -1559,13 +1560,19 @@
         block = pl.ds(i * size, size)
         copies.send(first_ids[i], first_own.at[block], first_other.at[block], place.other)
     first_back.halve()
+    fetch(out_core_landing.at[pl.ds(0, rows)], spare, sem)
+    add_to(out_sum.at[slot(0)], spare)
+    copies.receive(out_pair_id, out_pair_landing, place.pair)
+    fetch(out_pair_landing, spare, sem)
+    add_to(out_sum.at[slot(0)], spare)
+    copies.send(out_other_id, out_sum.at[slot(0)], out_other_landing, place.other)
     gate_backs[0].finish()
+    up_backs[1].line.step((-1,))
+    gate_backs[1].line.step((-1,))
     gate_backs[1].line.step((1,))
     wo_back.quarter()
     wo_back.line.start()
-    up_backs[1].line.step((-1,))
     first_back.quarter()
-    gate_backs[1].line.step((-1,))
     first_back.line.start()
     sum_take(0, place.other)
     sum_step(1, place.pair)
@@ -1702,6 +1709,8 @@
         vmem(4, batches, per_batch, 2 * head_size),
         vmem(4, batches, per_batch, 2 * head_size),
         vmem(own_rows, marks.shape[0], kind=wide_type),
+        vmem(rows, head_size, kind=wide_type),
+        vmem(rows, head_size, kind=wide_type),
         vmem(rows, 2, kind=wide_type),
         vmem(8, total_columns, kind=wide_type),
         vmem(4, sum_rows, LANES, kind=wide_type),
@@ -1714,7 +1723,7 @@
     results = pl.pallas_call(
         functools.partial(layer_kernel, heads, head_size),
         out_shape=[out[0] for out in outs] + list(kept),
-        in_specs=[in_vmem] + [anywhere] * 6 + [in_vmem] * 6,
+        in_specs=[in_vmem] + [anywhere] * 6 + [in_vmem] * 5,
         out_specs=[out[1] for out in outs] + [anywhere] * len(kept),
         scratch_shapes=scratch,
         compiler_params=pltpu.CompilerParams(
@@ -1773,9 +1782,11 @@
     row_start = place * count_rows
     rows = batches * count_rows
 
-    gains = jnp.stack([norm1_gain, norm2_gain], axis=1)
-    gains = jnp.pad(gains, ((0, 0), (0, LANES - 2)))
-    first_shard = jnp.concatenate([query_weight, key_weight, value_weight, gains], axis=1)
+    no_gain = jnp.zeros((norm1_gain.shape[0], LANES - 2), norm1_gain.dtype)
+    first_shard = jnp.concatenate(
+        [query_weight, key_weight, value_weight, norm1_gain[:, None], norm2_gain[:, None], no_gain],
+        axis=1,
+    )
     kv_width = query_width + 2 * head_size
     padded = -(-units // (4 * LANES)) * (4 * LANES)
 
@@ -1787,9 +1798,9 @@
     biases = jnp.concatenate(
         [query_bias.reshape(-1), key_bias.reshape(-1), value_bias.reshape(-1)]
     )
-    own_places = lax.dynamic_slice_in_dim(positions, row_start, count_rows, axis=1)
-    cosine, sine_table = rotation(own_places.reshape(-1), head_size)
     if lax.axis_size(RING) == LINE:
+        halves = np.arange(head_size // 2, dtype=np.float64)
+        frequency = (THETA ** (-2.0 * halves / head_size)).astype(np.float32)
         marks = jnp.concatenate([segments, positions]).astype(jnp.float32)
         lanes = -(-(BACK + 1) * count_rows // LANES) * LANES
         marks = jnp.pad(
@@ -1827,8 +1838,7 @@
                 query_bias,
                 key_bias,
                 value_bias,
-                cosine[:, 0],
-                sine_table[:, 0],
+                jnp.asarray(np.concatenate([frequency, frequency])[None]),
                 marks,
             ),
         )
@@ -1865,6 +1875,8 @@
             norm1_gain.shape[0],
         )
     else:
+        own_places = lax.dynamic_slice_in_dim(positions, row_start, count_rows, axis=1)
+        cosine, sine_table = rotation(own_places.reshape(-1), head_size)
         allowed = [
             visible(segments[b], positions[b], row_start, count_rows) for b in range(batches)
         ]

time: 401 us -> 400 us (level)
  other arithmetic: 5.56 us -> 0.78 us
where the time goes in v2:
time: 400 us; the launch traced here: 394 us
  Pallas kernels  389 us (97%)
    pallas_call x1, Pallas kernels, layer_call(): pl.pallas_call(functools.partial(layer_kernel, heads, head_size), out_sha...  382 us

profile of v2, /device:TPU:0, one launch (start us, length us, event | category | flops | bytes accessed | tf_op | source)
XLA Modules:
  0.0 394.5 jit_solution(1539770476160369540)
XLA Ops:
  0.7 0.8 copy.31
  1.4 0.8 copy.32
  2.2 0.8 add_convert_fusion
  3.0 0.7 pad_dynamic-slice_fusion.marks
  3.7 1.7 concatenate.6.first_shard
  5.4 382.0 %shard_map.272 = (bf16[384,1536]{1,0:T(8,128)(2,1)}, f32[384,1536]{1,0:T(8,128)}, f32[96,768]{1,0:T(8,128)}, f32[96,128]{1,0:T(8,128)}, f32[96,128]{1,0:T(8,128)...) custom-call(bf16[384,1536]{1,0:T(8,128)(2,1)} %bitcast.10, ...), custom_call_target="tpu_custom_call" | custom-call | tf_op jit(solution)/shard_map/pallas_call | solution.py:1723
  387.5 6.8 %shard_map.273 = (bf16[384,1536]{1,0:T(8,128)(2,1)}, f32[384,1536]{1,0:T(8,128)}, f32[96,768]{1,0:T(8,128)}, f32[96,128]{1,0:T(8,128)}, f32[96,128]{1,0:T(8,128)...) custom-call(bf16[384,1536]{1,0:T(8,128)(2,1)} %get-tuple-element.42., ...), custom_call_target="tpu_custom_call" | custom-call | tf_op jit(solution)/shard_map/pallas_call | solution.py:1750
  (1 shorter events, 0.0 us)
